TPU v7x, 32 devices: a whole 2x2x4 slice. The times are simulated.
32 devices in a mesh: pb: 8 (over z, x), lat: 4 (over y, core).
Axes of the slice: x: 2, y: 2, z: 4, core: 2. Of those that a mesh axis runs over, the one named last changes fastest.
Arguments:
- queries: bfloat16 [4096, 322], P('pb')
- tile_ids: int32 [4096], P('pb'), may hold values from 0 to 63
- tile_table: float32 [64, 322], replicated, may hold values from -6 to 6
- valid: int32 [4096], P(('pb', 'lat')), may hold values 0 or 1
- latents: bfloat16 [16384, 512], P(('pb', 'lat')), may hold values from -6 to 6
- lat_gain: float32 [512], replicated, may hold values from 0.25 to 1.75
- query_gain: float32 [322], replicated, may hold values from 0.25 to 1.75
- w_query: bfloat16 [322, 512], replicated, may hold values from -64 to 64
- w_key: bfloat16 [512, 512], replicated, may hold values from -0.25 to 0.25
- w_value: bfloat16 [512, 512], replicated, may hold values from -0.25 to 0.25
- w_out: bfloat16 [512, 322], replicated, may hold values from -0.25 to 0.25
- mlp_gain: float32 [322], replicated, may hold values from 0.25 to 1.75
- w_hidden: bfloat16 [322, 322], replicated, may hold values from -0.3125 to 0.3125
- w_back: bfloat16 [322, 322], replicated, may hold values from -0.3125 to 0.3125
- w_flow: bfloat16 [2, 322], replicated, may hold values from -0.3125 to 0.3125
Outputs:
- flow: float32 [2, 4096], P(None, ('pb', 'lat'))
All inputs are finite; a program needn't handle non-finite values. No bound on the sum of `valid` on one device may be relied on, other than what follows from the above.
Results may differ from a plain program's by a relative error of at most 0.04.
Values may be sent and summed in bfloat16 or wider, within the bound.
A program may use at most 128 MiB of HBM per device.

v0:
```python
import math

import jax
import jax.numpy as jnp
from jax import lax
from jax.sharding import PartitionSpec as P

HEADS = 8
DH = 64


def combined_all(shard, axis, combine):
    everything = jax.tree.map(lambda part: lax.all_gather(part, axis), shard)
    initial = jax.tree.map(lambda part: part[0], everything)

    def turn(k, so_far):
        return combine(so_far, jax.tree.map(lambda part: part[k], everything))

    return lax.fori_loop(1, lax.axis_size(axis), turn, initial)


def layer_norm(values, gain):
    center = values - jnp.mean(values, axis=-1, keepdims=True)
    spread = jnp.mean(center * center, axis=-1, keepdims=True)
    return center * lax.rsqrt(spread + 1e-05) * gain


def attend_rows(carry, query_heads, keys, values):
    rows = keys.shape[0]
    step_rows = math.gcd(rows, 256)
    heads = query_heads.shape[0]
    width = query_heads.shape[2]
    key_blocks = keys.reshape(rows // step_rows, step_rows, heads, width)
    value_blocks = values.reshape(rows // step_rows, step_rows, heads, width)

    def update(state, block):
        top, total, mixed = state
        key_part, value_part = block
        scores = (
            jnp.einsum("hqd,khd->hqk", query_heads, key_part, preferred_element_type=jnp.float32)
            * 0.125
        )
        new_top = jnp.maximum(top, jnp.max(scores, axis=-1))
        weights = jnp.exp(scores - new_top[:, :, None])
        factor = jnp.exp(top - new_top)
        total = total * factor + jnp.sum(weights, axis=-1)
        mixed = mixed * factor[:, :, None] + jnp.einsum(
            "hqk,khd->hqd",
            weights.astype(jnp.bfloat16),
            value_part,
            preferred_element_type=jnp.float32,
        )
        return ((new_top, total, mixed), None)

    result, unused = lax.scan(update, carry, (key_blocks, value_blocks))
    return result


def combine_parts(first, second):
    top = jnp.maximum(first[0], second[0])
    left = jnp.exp(first[0] - top)
    right = jnp.exp(second[0] - top)
    return (
        top,
        first[1] * left + second[1] * right,
        first[2] * left[:, :, None] + second[2] * right[:, :, None],
    )


def local(
    queries,
    tile_ids,
    tile_table,
    valid,
    latents,
    lat_gain,
    query_gain,
    w_query,
    w_key,
    w_value,
    w_out,
    mlp_gain,
    w_hidden,
    w_back,
    w_flow,
):
    rows = queries.shape[0]
    heads = HEADS
    width = DH
    tiles = tile_table.shape[0]
    onehot = (tile_ids[:, None] == jnp.arange(tiles, dtype=jnp.int32)[None, :]).astype(jnp.float32)
    shifted = queries.astype(jnp.float32) + jnp.dot(
        onehot, tile_table, precision=lax.Precision.HIGHEST
    )
    normed = layer_norm(shifted, query_gain).astype(jnp.bfloat16)
    query_proj = jnp.dot(normed, w_query, preferred_element_type=jnp.float32).astype(jnp.bfloat16)
    query_heads = jnp.transpose(query_proj.reshape(rows, heads, width), (1, 0, 2))
    lat_normed = layer_norm(latents.astype(jnp.float32), lat_gain).astype(jnp.bfloat16)
    start_state = (
        jnp.full((heads, rows), -1e30, jnp.float32),
        jnp.zeros((heads, rows), jnp.float32),
        jnp.zeros((heads, rows, width), jnp.float32),
    )
    piece = lax.all_gather(lat_normed, "pb", axis=0, tiled=True)
    count = piece.shape[0]
    keys = jnp.dot(piece, w_key, preferred_element_type=jnp.float32).astype(jnp.bfloat16)
    values = jnp.dot(piece, w_value, preferred_element_type=jnp.float32).astype(jnp.bfloat16)
    state = attend_rows(
        start_state,
        query_heads,
        keys.reshape(count, heads, width),
        values.reshape(count, heads, width),
    )
    top, total, mixed = combined_all(state, "lat", combine_parts)
    share = rows // lax.axis_size("lat")
    begin = lax.axis_index("lat") * share
    mixed = lax.dynamic_slice_in_dim(mixed, begin, share, 1)
    total = lax.dynamic_slice_in_dim(total, begin, share, 1)
    attn = (
        jnp.transpose(mixed / total[:, :, None], (1, 0, 2))
        .reshape(share, heads * width)
        .astype(jnp.bfloat16)
    )
    projected = jnp.dot(attn, w_out, preferred_element_type=jnp.float32)
    normed_two = layer_norm(projected, mlp_gain)
    hidden = jax.nn.gelu(
        jnp.dot(normed_two.astype(jnp.bfloat16), w_hidden, preferred_element_type=jnp.float32),
        approximate=False,
    ).astype(jnp.bfloat16)
    updated = (normed_two + jnp.dot(hidden, w_back, preferred_element_type=jnp.float32)).astype(
        jnp.bfloat16
    )
    flow = lax.dot_general(
        w_flow, updated, (((1,), (1,)), ((), ())), preferred_element_type=jnp.float32
    )
    return flow * valid.astype(jnp.float32)[None, :]


def solution(mesh):
    placed = (
        P("pb", None),
        P("pb"),
        P(),
        P(("pb", "lat")),
        P(("pb", "lat"), None),
        P(),
        P(),
        P(),
        P(),
        P(),
        P(),
        P(),
        P(),
        P(),
        P(),
    )
    return jax.shard_map(
        local, mesh=mesh, in_specs=placed, out_specs=P(None, ("pb", "lat")), check_vma=False
    )
```

profile of v0, /device:TPU:0, one launch (start us, length us, event | category | flops | bytes accessed | tf_op | source)
XLA Modules:
  0.0 359.9 jit_solution(16978859386622988791)
XLA Ops:
  9.2 2.1 fusion.30
  13.7 73.8 %all-gather.6.cloned.1.call-done = bf16[4096,512]{1,0:T(8,128)(2,1)} async-done(((bf16[512,512]{1,0:T(8,128)(2,1)}), bf16[4096,512]{1,0:T(8,128)(2,1)}) %all-gather.6.cloned.1.call-update) | async-done | bytes 4194320 | tf_op jit(solution)/shard_map/all_gather | solution.py:104
  87.5 6.5 %convolution_convert_fusion.1 = bf16[4096,512]{1,0:T(8,128)(2,1)} fusion(bf16[4096,512]{1,0:T(8,128)(2,1)} %all-gather.6.cloned.1.call-done, bf16[512,512]{1,0:T(8,128)(2,1)S(1)} %copy-done), kind=kOutput, calls=%fused_computation.32 | convolution fusion | flops 2149580800 | bytes 8912896 | tf_op jit(solution)/shard_map/dot_general | solution.py:106
  94.0 11.2 %reshape.61 = bf16[16,256,8,64]{3,2,1,0:T(8,128)(2,1)} reshape(bf16[4096,512]{1,0:T(8,128)(2,1)} %convolution_convert_fusion.1) | data formatting | bytes 8388608 | tf_op jit(solution)/shard_map/reshape;reshape | solution.py:33
  105.2 9.2 %copy.32 = bf16[16,256,8,64]{1,3,2,0:T(8,128)(2,1)} copy(bf16[16,256,8,64]{3,2,1,0:T(8,128)(2,1)} %reshape.61) | data formatting | bytes 8388608
  114.4 6.5 %convolution_convert_fusion = bf16[4096,512]{1,0:T(8,128)(2,1)} fusion(bf16[4096,512]{1,0:T(8,128)(2,1)} %all-gather.6.cloned.1.call-done, bf16[512,512]{1,0:T(8,128)(2,1)S(1)} %copy-done.8), kind=kOutput, calls=%fused_computation.31 | convolution fusion | flops 2149580800 | bytes 8912896 | tf_op jit(solution)/shard_map/dot_general | solution.py:107
  120.8 11.2 %reshape.62 = bf16[16,256,8,64]{3,2,1,0:T(8,128)(2,1)} reshape(bf16[4096,512]{1,0:T(8,128)(2,1)} %convolution_convert_fusion) | data formatting | bytes 8388608 | tf_op jit(solution)/shard_map/reshape;reshape | solution.py:34
  132.0 9.1 %copy.33 = bf16[16,256,8,64]{1,3,2,0:T(8,128)(2,1)} copy(bf16[16,256,8,64]{3,2,1,0:T(8,128)(2,1)} %reshape.62) | data formatting | bytes 8388608
  141.1 144.8 %while.35 = (s32[]{:T(128)}, f32[8,512]{1,0:T(8,128)S(1)}, f32[8,512]{1,0:T(8,128)S(1)}, f32[8,512,64]{1,2,0:T(8,128)S(1)}, bf16[16,256,8,64]{1,3,2,0:T(8,128)(2...) while((s32[]{:T(128)}, f32[8,512]{1,0:T(8,128)S(1)}, ...), condition=%wide.region_7.8_spmd.clone, body=%wide.region_4.7_spmd.clone.sunk | while | flops 277630976 | bytes 32769156 | solution.py:55
  141.1 3.7 %bitcast_reduce_fusion.2 = (f32[8,512]{1,0:T(8,128)S(1)}, f32[8,256,512]{2,1,0:T(8,128)}) fusion(bf16[8,512,64]{1,2,0:T(8,128)(2,1)S(1)} %get-tuple-element.457, bf16[16,256,8,64]{1,3,2,0:T(8,128)(2,1)} %get-tuple-element.456, s32[]{:T(128)} %get-tuple-element.443), kind=kOutput, calls=%fused_computation.10.clone.1 | convolution fusion | flops 136310784 | bytes 4997632 | tf_op jit(solution)/shard_map/while/body/eval_jaxpr/hqd,khd->hqk/dot_general | solution.py:40
  144.8 3.1 fusion.204
  150.2 3.6 %bitcast_reduce_fusion.2 = (f32[8,512]{1,0:T(8,128)S(1)}, f32[8,256,512]{2,1,0:T(8,128)}) fusion(bf16[8,512,64]{1,2,0:T(8,128)(2,1)S(1)} %get-tuple-element.457, bf16[16,256,8,64]{1,3,2,0:T(8,128)(2,1)} %get-tuple-element.456, s32[]{:T(128)} %get-tuple-element.443), kind=kOutput, calls=%fused_computation.10.clone.1 | convolution fusion | flops 136310784 | bytes 4997632 | tf_op jit(solution)/shard_map/while/body/eval_jaxpr/hqd,khd->hqk/dot_general | solution.py:40
  153.8 3.1 fusion.204
  159.2 3.6 %bitcast_reduce_fusion.2 = (f32[8,512]{1,0:T(8,128)S(1)}, f32[8,256,512]{2,1,0:T(8,128)}) fusion(bf16[8,512,64]{1,2,0:T(8,128)(2,1)S(1)} %get-tuple-element.457, bf16[16,256,8,64]{1,3,2,0:T(8,128)(2,1)} %get-tuple-element.456, s32[]{:T(128)} %get-tuple-element.443), kind=kOutput, calls=%fused_computation.10.clone.1 | convolution fusion | flops 136310784 | bytes 4997632 | tf_op jit(solution)/shard_map/while/body/eval_jaxpr/hqd,khd->hqk/dot_general | solution.py:40
  162.9 3.1 fusion.204
  166.3 1.9 fusion.206
  168.3 3.6 %bitcast_reduce_fusion.2 = (f32[8,512]{1,0:T(8,128)S(1)}, f32[8,256,512]{2,1,0:T(8,128)}) fusion(bf16[8,512,64]{1,2,0:T(8,128)(2,1)S(1)} %get-tuple-element.457, bf16[16,256,8,64]{1,3,2,0:T(8,128)(2,1)} %get-tuple-element.456, s32[]{:T(128)} %get-tuple-element.443), kind=kOutput, calls=%fused_computation.10.clone.1 | convolution fusion | flops 136310784 | bytes 4997632 | tf_op jit(solution)/shard_map/while/body/eval_jaxpr/hqd,khd->hqk/dot_general | solution.py:40
  172.0 3.1 fusion.204
  175.4 1.9 fusion.206
  177.3 3.6 %bitcast_reduce_fusion.2 = (f32[8,512]{1,0:T(8,128)S(1)}, f32[8,256,512]{2,1,0:T(8,128)}) fusion(bf16[8,512,64]{1,2,0:T(8,128)(2,1)S(1)} %get-tuple-element.457, bf16[16,256,8,64]{1,3,2,0:T(8,128)(2,1)} %get-tuple-element.456, s32[]{:T(128)} %get-tuple-element.443), kind=kOutput, calls=%fused_computation.10.clone.1 | convolution fusion | flops 136310784 | bytes 4997632 | tf_op jit(solution)/shard_map/while/body/eval_jaxpr/hqd,khd->hqk/dot_general | solution.py:40
  181.0 3.1 fusion.204
  184.4 1.9 fusion.206
  186.4 3.6 %bitcast_reduce_fusion.2 = (f32[8,512]{1,0:T(8,128)S(1)}, f32[8,256,512]{2,1,0:T(8,128)}) fusion(bf16[8,512,64]{1,2,0:T(8,128)(2,1)S(1)} %get-tuple-element.457, bf16[16,256,8,64]{1,3,2,0:T(8,128)(2,1)} %get-tuple-element.456, s32[]{:T(128)} %get-tuple-element.443), kind=kOutput, calls=%fused_computation.10.clone.1 | convolution fusion | flops 136310784 | bytes 4997632 | tf_op jit(solution)/shard_map/while/body/eval_jaxpr/hqd,khd->hqk/dot_general | solution.py:40
  190.1 3.1 fusion.204
  193.5 1.9 fusion.206
  195.5 3.6 %bitcast_reduce_fusion.2 = (f32[8,512]{1,0:T(8,128)S(1)}, f32[8,256,512]{2,1,0:T(8,128)}) fusion(bf16[8,512,64]{1,2,0:T(8,128)(2,1)S(1)} %get-tuple-element.457, bf16[16,256,8,64]{1,3,2,0:T(8,128)(2,1)} %get-tuple-element.456, s32[]{:T(128)} %get-tuple-element.443), kind=kOutput, calls=%fused_computation.10.clone.1 | convolution fusion | flops 136310784 | bytes 4997632 | tf_op jit(solution)/shard_map/while/body/eval_jaxpr/hqd,khd->hqk/dot_general | solution.py:40
  199.1 3.1 fusion.204
  202.6 1.9 fusion.206
  204.5 3.6 %bitcast_reduce_fusion.2 = (f32[8,512]{1,0:T(8,128)S(1)}, f32[8,256,512]{2,1,0:T(8,128)}) fusion(bf16[8,512,64]{1,2,0:T(8,128)(2,1)S(1)} %get-tuple-element.457, bf16[16,256,8,64]{1,3,2,0:T(8,128)(2,1)} %get-tuple-element.456, s32[]{:T(128)} %get-tuple-element.443), kind=kOutput, calls=%fused_computation.10.clone.1 | convolution fusion | flops 136310784 | bytes 4997632 | tf_op jit(solution)/shard_map/while/body/eval_jaxpr/hqd,khd->hqk/dot_general | solution.py:40
  208.2 3.1 fusion.204
  211.6 1.9 fusion.206
  213.6 3.6 %bitcast_reduce_fusion.2 = (f32[8,512]{1,0:T(8,128)S(1)}, f32[8,256,512]{2,1,0:T(8,128)}) fusion(bf16[8,512,64]{1,2,0:T(8,128)(2,1)S(1)} %get-tuple-element.457, bf16[16,256,8,64]{1,3,2,0:T(8,128)(2,1)} %get-tuple-element.456, s32[]{:T(128)} %get-tuple-element.443), kind=kOutput, calls=%fused_computation.10.clone.1 | convolution fusion | flops 136310784 | bytes 4997632 | tf_op jit(solution)/shard_map/while/body/eval_jaxpr/hqd,khd->hqk/dot_general | solution.py:40
  217.2 3.1 fusion.204
  220.7 1.9 fusion.206
  222.6 3.6 %bitcast_reduce_fusion.2 = (f32[8,512]{1,0:T(8,128)S(1)}, f32[8,256,512]{2,1,0:T(8,128)}) fusion(bf16[8,512,64]{1,2,0:T(8,128)(2,1)S(1)} %get-tuple-element.457, bf16[16,256,8,64]{1,3,2,0:T(8,128)(2,1)} %get-tuple-element.456, s32[]{:T(128)} %get-tuple-element.443), kind=kOutput, calls=%fused_computation.10.clone.1 | convolution fusion | flops 136310784 | bytes 4997632 | tf_op jit(solution)/shard_map/while/body/eval_jaxpr/hqd,khd->hqk/dot_general | solution.py:40
  226.3 3.1 fusion.204
  231.7 3.6 %bitcast_reduce_fusion.2 = (f32[8,512]{1,0:T(8,128)S(1)}, f32[8,256,512]{2,1,0:T(8,128)}) fusion(bf16[8,512,64]{1,2,0:T(8,128)(2,1)S(1)} %get-tuple-element.457, bf16[16,256,8,64]{1,3,2,0:T(8,128)(2,1)} %get-tuple-element.456, s32[]{:T(128)} %get-tuple-element.443), kind=kOutput, calls=%fused_computation.10.clone.1 | convolution fusion | flops 136310784 | bytes 4997632 | tf_op jit(solution)/shard_map/while/body/eval_jaxpr/hqd,khd->hqk/dot_general | solution.py:40
  235.3 3.1 fusion.204
  238.8 1.9 fusion.206
  240.7 3.6 %bitcast_reduce_fusion.2 = (f32[8,512]{1,0:T(8,128)S(1)}, f32[8,256,512]{2,1,0:T(8,128)}) fusion(bf16[8,512,64]{1,2,0:T(8,128)(2,1)S(1)} %get-tuple-element.457, bf16[16,256,8,64]{1,3,2,0:T(8,128)(2,1)} %get-tuple-element.456, s32[]{:T(128)} %get-tuple-element.443), kind=kOutput, calls=%fused_computation.10.clone.1 | convolution fusion | flops 136310784 | bytes 4997632 | tf_op jit(solution)/shard_map/while/body/eval_jaxpr/hqd,khd->hqk/dot_general | solution.py:40
  244.4 3.1 fusion.204
  249.8 3.6 %bitcast_reduce_fusion.2 = (f32[8,512]{1,0:T(8,128)S(1)}, f32[8,256,512]{2,1,0:T(8,128)}) fusion(bf16[8,512,64]{1,2,0:T(8,128)(2,1)S(1)} %get-tuple-element.457, bf16[16,256,8,64]{1,3,2,0:T(8,128)(2,1)} %get-tuple-element.456, s32[]{:T(128)} %get-tuple-element.443), kind=kOutput, calls=%fused_computation.10.clone.1 | convolution fusion | flops 136310784 | bytes 4997632 | tf_op jit(solution)/shard_map/while/body/eval_jaxpr/hqd,khd->hqk/dot_general | solution.py:40
  253.4 3.1 fusion.204
  256.9 1.9 fusion.206
  258.8 3.6 %bitcast_reduce_fusion.2 = (f32[8,512]{1,0:T(8,128)S(1)}, f32[8,256,512]{2,1,0:T(8,128)}) fusion(bf16[8,512,64]{1,2,0:T(8,128)(2,1)S(1)} %get-tuple-element.457, bf16[16,256,8,64]{1,3,2,0:T(8,128)(2,1)} %get-tuple-element.456, s32[]{:T(128)} %get-tuple-element.443), kind=kOutput, calls=%fused_computation.10.clone.1 | convolution fusion | flops 136310784 | bytes 4997632 | tf_op jit(solution)/shard_map/while/body/eval_jaxpr/hqd,khd->hqk/dot_general | solution.py:40
  262.5 3.1 fusion.204
  267.9 3.6 %bitcast_reduce_fusion.2 = (f32[8,512]{1,0:T(8,128)S(1)}, f32[8,256,512]{2,1,0:T(8,128)}) fusion(bf16[8,512,64]{1,2,0:T(8,128)(2,1)S(1)} %get-tuple-element.457, bf16[16,256,8,64]{1,3,2,0:T(8,128)(2,1)} %get-tuple-element.456, s32[]{:T(128)} %get-tuple-element.443), kind=kOutput, calls=%fused_computation.10.clone.1 | convolution fusion | flops 136310784 | bytes 4997632 | tf_op jit(solution)/shard_map/while/body/eval_jaxpr/hqd,khd->hqk/dot_general | solution.py:40
  271.5 3.1 fusion.204
  275.0 1.9 fusion.206
  276.9 3.6 %bitcast_reduce_fusion.2 = (f32[8,512]{1,0:T(8,128)S(1)}, f32[8,256,512]{2,1,0:T(8,128)}) fusion(bf16[8,512,64]{1,2,0:T(8,128)(2,1)S(1)} %get-tuple-element.457, bf16[16,256,8,64]{1,3,2,0:T(8,128)(2,1)} %get-tuple-element.456, s32[]{:T(128)} %get-tuple-element.443), kind=kOutput, calls=%fused_computation.10.clone.1 | convolution fusion | flops 136310784 | bytes 4997632 | tf_op jit(solution)/shard_map/while/body/eval_jaxpr/hqd,khd->hqk/dot_general | solution.py:40
  280.6 3.1 fusion.204
  284.0 1.9 fusion.206
  287.0 5.2 %all-gather = f32[32,512]{1,0:T(8,128)S(1)} all-gather(f32[8,512]{1,0:T(8,128)S(1)} %get-tuple-element.221), channel_id=2, replica_groups=mesh['pb'=8,'lat'=4] {'lat'}, dimensions={0}, use_global_device_ids=true | all-gather | bytes 81920 | tf_op jit(solution)/shard_map/all_gather | solution.py:13
  292.2 5.4 %all-gather.1 = f32[32,512]{1,0:T(8,128)S(1)} all-gather(f32[8,512]{1,0:T(8,128)S(1)} %get-tuple-element.222), channel_id=3, replica_groups=mesh['pb'=8,'lat'=4] {'lat'}, dimensions={0}, use_global_device_ids=true | all-gather | bytes 81920 | tf_op jit(solution)/shard_map/all_gather | solution.py:13
  297.7 22.6 %all-gather.8.cloned.1.call-done = f32[32,512,64]{1,2,0:T(8,128)} async-done(((f32[8,512,64]{1,2,0:T(8,128)}), f32[32,512,64]{1,2,0:T(8,128)}) %all-gather.8.cloned.1.call-update) | async-done | bytes 4194320 | tf_op jit(solution)/shard_map/all_gather | solution.py:13
  321.6 1.9 copy.34
  323.5 25.2 %while.34 = (s32[]{:T(128)}, f32[8,512]{1,0:T(8,128)S(1)}, f32[8,512]{1,0:T(8,128)S(1)}, f32[8,512,64]{2,1,0:T(8,128)}, f32[4,8,512]{2,1,0:T(8,128)S(1)}, /*inde...) while((s32[]{:T(128)}, f32[8,512]{1,0:T(8,128)S(1)}, ...), condition=%wide.region_9.10_spmd, body=%wide.region_8.9_spmd.sunk | while | flops 811013 | bytes 7504023 | solution.py:19
  323.5 2.3 constant_dynamic-slice_fusion.3
  327.7 4.2 %fusion.200 = f32[8,512,64]{2,1,0:T(8,128)} fusion(f32[1,8,512,64]{3,2,1,0:T(8,128)S(1)} %copy.44, f32[8,512,64]{2,1,0:T(8,128)} %get-tuple-element.474, f32[8,512]{1,0:T(8,128)S(1)} %get-tuple-element.421, f32[8,512]{1,0:T(8,128)S(1)} %get-tuple-element.422), kind=kLoop, calls=%fused_computation.1.clone.1 | loop fusion | flops 786432 | bytes 3178496 | tf_op jit(solution)/shard_map/while/body/eval_jaxpr/add | solution.py:66
  331.9 2.3 constant_dynamic-slice_fusion.3
  336.1 4.2 %fusion.200 = f32[8,512,64]{2,1,0:T(8,128)} fusion(f32[1,8,512,64]{3,2,1,0:T(8,128)S(1)} %copy.44, f32[8,512,64]{2,1,0:T(8,128)} %get-tuple-element.474, f32[8,512]{1,0:T(8,128)S(1)} %get-tuple-element.421, f32[8,512]{1,0:T(8,128)S(1)} %get-tuple-element.422), kind=kLoop, calls=%fused_computation.1.clone.1 | loop fusion | flops 786432 | bytes 3178496 | tf_op jit(solution)/shard_map/while/body/eval_jaxpr/add | solution.py:66
  340.3 2.3 constant_dynamic-slice_fusion.3
  344.4 4.2 %fusion.200 = f32[8,512,64]{2,1,0:T(8,128)} fusion(f32[1,8,512,64]{3,2,1,0:T(8,128)S(1)} %copy.44, f32[8,512,64]{2,1,0:T(8,128)} %get-tuple-element.474, f32[8,512]{1,0:T(8,128)S(1)} %get-tuple-element.421, f32[8,512]{1,0:T(8,128)S(1)} %get-tuple-element.422), kind=kLoop, calls=%fused_computation.1.clone.1 | loop fusion | flops 786432 | bytes 3178496 | tf_op jit(solution)/shard_map/while/body/eval_jaxpr/add | solution.py:66
  348.7 2.2 copy.36
  (141 shorter events, 30.6 us)
Async XLA Ops:
  6.5 81.0 %copy-start = (bf16[512,512]{1,0:T(8,128)(2,1)S(1)}, bf16[512,512]{1,0:T(8,128)(2,1)}, u32[]{:S(2)}) copy-start(bf16[512,512]{1,0:T(8,128)(2,1)} %param.27) | copy-start | bytes 1572868
  6.5 6.6 %copy-start.6 = (f32[322]{0:T(512)S(1)}, f32[322]{0:T(512)}, u32[]{:S(2)}) copy-start(f32[322]{0:T(512)} %param.25) | copy-start | bytes 3868
  6.5 6.6 %copy-start.3 = (bf16[322,512]{1,0:T(8,128)(2,1)S(1)}, bf16[322,512]{1,0:T(8,128)(2,1)}, u32[]{:S(2)}) copy-start(bf16[322,512]{1,0:T(8,128)(2,1)} %param.26) | copy-start | bytes 989188
  6.5 81.0 %all-gather.6.cloned.1.call-start = ((), (), s32[]{:S(2)}) async-start(), calls=%async_computation | async-start | bytes 4718592 | tf_op jit(solution)/shard_map/all_gather | solution.py:104
  11.3 309.0 %all-gather.8.cloned.1.call-start = ((), (), s32[]{:S(2)}) async-start(), calls=%async_computation.1 | async-start | bytes 5242880 | tf_op jit(solution)/shard_map/all_gather | solution.py:13
  105.2 9.2 %copy-start.8 = (bf16[512,512]{1,0:T(8,128)(2,1)S(1)}, bf16[512,512]{1,0:T(8,128)(2,1)}, u32[]{:S(2)}) copy-start(bf16[512,512]{1,0:T(8,128)(2,1)} %param.28) | copy-start | bytes 1572868
  141.1 145.8 %copy-start.11 = (s32[128]{0:T(128)S(1)}, s32[128]{0:T(128)}, u32[]{:S(2)}) copy-start(s32[128]{0:T(128)} %param.22) | copy-start | bytes 1540
  144.8 3.4 copy-start.1
  153.8 3.4 copy-start.1
  162.9 3.4 copy-start.1
  171.9 3.4 copy-start.1
  181.0 3.4 copy-start.1
  190.0 3.4 copy-start.1
  199.1 3.4 copy-start.1
  208.2 3.4 copy-start.1
  217.2 3.4 copy-start.1
  226.3 3.4 copy-start.1
  235.3 3.4 copy-start.1
  244.4 3.4 copy-start.1
  253.4 3.4 copy-start.1
  262.5 3.4 copy-start.1
  271.5 3.4 copy-start.1
  280.6 3.4 copy-start.1
  286.0 1.0 copy-start.2
  323.5 27.5 %copy-start.4 = (bf16[512,322]{0,1:T(8,128)(2,1)S(1)}, bf16[512,322]{0,1:T(8,128)(2,1)}, u32[]{:S(2)}) copy-start(bf16[512,322]{0,1:T(8,128)(2,1)} %param.29) | copy-start | bytes 989188
  348.7 2.7 copy-start.5
  348.7 2.7 copy-start.7
  348.7 3.1 copy-start.9
  348.7 3.1 copy-start.10
Sparse Core Ops, SparseCore 0:
  11.4 76.0 all-gather.5
  287.1 33.0 all-gather.7
where the time goes:
time: 362 us; the launch traced here: 360 us
  matrix products  106 us (29%)
  waiting for transfers between devices  96.4 us (27%)
  other arithmetic  66.8 us (18%)
  local copies, waits for them, and re-layouts  65.4 us (18%)
  between operations  13.6 us (4%)
  blocking collectives  10.7 us (3%)
    all_gather x1, waiting for transfers between devices, local(): piece = lax.all_gather(lat_normed, 'pb', axis=0, tiled=True)  73.8 us
    dot_general x16, matrix products, update(): jnp.einsum('hqd,khd->hqk', query_heads, key_part, preferred_element_type=...  58.3 us
    reduce_sum x16, other arithmetic, update(): total = total * factor + jnp.sum(weights, axis=-1)  48.8 us
    dot_general x16, matrix products, update(): jnp.einsum('hqk,khd->hqd', weights.astype(jnp.bfloat16), value_part, pref...  30.8 us
    all_gather x1, waiting for transfers between devices, combined_all(): everything = jax.tree.map(lambda part: lax.all_gather(part, axis), shard)  22.6 us
    unnamed x24, local copies, waits for them, and re-layouts  19.3 us
    add x3, other arithmetic, combine_parts(): first[2] * left[:, :, None] + second[2] * right[:, :, None]  12.7 us
    dynamic_slice x6, local copies, waits for them, and re-layouts, turn(): return combine(so_far, jax.tree.map(lambda part: part[k], everything))  12.4 us
  transfers between devices with their start and end apart: 2, of which 2 were waited for; matrix products, arithmetic and copies ran while one was open for 1% of the time, Pallas kernels for 0%

commit v1 on v0

v1 whole, which is shorter than its diff:
```python
import functools
import math

import jax
import jax.numpy as jnp
from jax import lax
from jax.experimental import pallas as pl
from jax.experimental.pallas import tpu as pltpu
from jax.sharding import PartitionSpec as P

HEADS = 8
DH = 64
PAIR = 2 * DH
PAIRS = HEADS // 2
NEG = -1e30
BF = jnp.bfloat16
F32 = jnp.float32
VMEM = pl.BlockSpec(memory_space=pltpu.VMEM)


def layer_norm(values, gain):
    center = values - jnp.mean(values, axis=-1, keepdims=True)
    spread = jnp.mean(center * center, axis=-1, keepdims=True)
    return center * lax.rsqrt(spread + 1e-05) * gain


def prepare_kernel(part_ref, queries, ids, table, latents, lat_gain, query_gain, w_query, q_out, lat_out):
    tiles = table.shape[0]
    rows = queries.shape[0]
    lanes = lax.broadcasted_iota(jnp.int32, (rows, tiles), 1)
    onehot = (ids[...] == lanes).astype(F32)
    shifted = queries[...].astype(F32) + jnp.dot(
        onehot, table[...], precision=lax.Precision.HIGHEST, preferred_element_type=F32
    )
    normed = layer_norm(shifted, query_gain[...]).astype(BF)
    q = jnp.dot(normed, w_query[...], preferred_element_type=F32).astype(BF)
    q_out[...] = (q.astype(F32) * (DH ** -0.5)).astype(BF)
    lat_out[...] = layer_norm(latents[...].astype(F32), lat_gain[...]).astype(BF)


def attend_kernel(parts, pieces, first, last, *refs):
    refs = list(refs)
    q_refs = [refs.pop(0) for _ in range(parts)]
    lat_refs = [refs.pop(0) for _ in range(pieces)]
    w_key, w_value = refs.pop(0), refs.pop(0)
    if not first:
        acc_in, ml_in = refs.pop(0), refs.pop(0)
    if last:
        out = refs.pop(0)
    else:
        acc_out, ml_out = refs.pop(0), refs.pop(0)
    qm, keys, vals, = refs[:3]
    if last:
        acc_out, ml_out = refs[3:5]
    share = q_refs[0].shape[0]
    rows = share * parts
    count = keys.shape[1]
    low = lax.broadcasted_iota(jnp.int32, (share, PAIR), 1) < DH
    for k in range(parts):
        for p in range(PAIRS):
            both = q_refs[k][:, p * PAIR:(p + 1) * PAIR]
            zero = jnp.zeros_like(both)
            qm[2 * p, k * share:(k + 1) * share, :] = jnp.where(low, both, zero)
            qm[2 * p + 1, k * share:(k + 1) * share, :] = jnp.where(low, zero, both)
    at = 0
    for ref in lat_refs:
        n = ref.shape[0]
        piece = ref[...]
        kk = jnp.dot(piece, w_key[...], preferred_element_type=F32).astype(BF)
        vv = jnp.dot(piece, w_value[...], preferred_element_type=F32).astype(BF)
        for p in range(PAIRS):
            keys[p, at:at + n, :] = kk[:, p * PAIR:(p + 1) * PAIR]
            vals[p, at:at + n, :PAIR] = vv[:, p * PAIR:(p + 1) * PAIR]
            vals[p, at:at + n, PAIR:] = jnp.ones((n, PAIR), BF)
        at += n
    qrows = math.gcd(rows, 256)
    half = lax.broadcasted_iota(jnp.int32, (qrows, PAIR), 1) < DH

    def pair_step(p, unused):
        for c in range(rows // qrows):
            sl = slice(c * qrows, (c + 1) * qrows)
            mixed = []
            factors = []
            for h in range(2):
                s = lax.dot_general(
                    qm[2 * p + h, sl, :], keys[p], (((1,), (1,)), ((), ())),
                    preferred_element_type=F32,
                )
                top = jnp.max(s, axis=-1, keepdims=True)
                if not first:
                    old = ml_in[2 * p + h, sl, 0:1]
                    top = jnp.maximum(top, old)
                w = jnp.exp(s - top).astype(BF)
                r = jnp.dot(w, vals[p], preferred_element_type=F32)
                total = r[:, PAIR:]
                mixed.append(r[:, :PAIR])
                if not first:
                    factor = jnp.exp(old - top)
                    factors.append(factor)
                    total = total + factor * ml_in[2 * p + h, sl, DH:DH + 1]
                ml_out[2 * p + h, sl, :] = jnp.where(half, top, total)
            new = jnp.where(half, mixed[0], mixed[1])
            if not first:
                new = new + acc_in[p, sl, :] * jnp.where(half, factors[0], factors[1])
            acc_out[p, sl, :] = new
        return unused

    lax.fori_loop(0, PAIRS, pair_step, 0)
    if last:
        lane = lax.broadcasted_iota(jnp.int32, (qrows, PAIR), 1)
        for c in range(rows // qrows):
            sl = slice(c * qrows, (c + 1) * qrows)
            stats = jnp.zeros((qrows, PAIR), F32)
            for p in range(PAIRS):
                sums = []
                for h in range(2):
                    g = 2 * p + h
                    top = ml_out[g, sl, 0:1]
                    total = ml_out[g, sl, DH:DH + 1]
                    sums.append(total)
                    level = top + jnp.log(total)
                    hi = level.astype(BF).astype(F32)
                    mid = (level - hi).astype(BF).astype(F32)
                    lo = level - hi - mid
                    stats = jnp.where(lane == g, hi, stats)
                    stats = jnp.where(lane == HEADS + g, mid, stats)
                    stats = jnp.where(lane == 2 * HEADS + g, lo, stats)
                out[sl, p * PAIR:(p + 1) * PAIR] = (
                    acc_out[p, sl, :] / jnp.where(half, sums[0], sums[1])
                ).astype(BF)
            out[sl, PAIRS * PAIR:] = stats.astype(BF)


def attend(q_parts, pieces, w_key, w_value, state, last):
    first = state is None
    rows = sum(q.shape[0] for q in q_parts)
    count = sum(p.shape[0] for p in pieces)
    acc = jax.ShapeDtypeStruct((PAIRS, rows, PAIR), F32)
    ml = jax.ShapeDtypeStruct((HEADS, rows, PAIR), F32)
    packed = jax.ShapeDtypeStruct((rows, (PAIRS + 1) * PAIR), BF)
    args = [*q_parts, *pieces, w_key, w_value] + ([] if first else list(state))
    scratch = [
        pltpu.VMEM((HEADS, rows, PAIR), BF),
        pltpu.VMEM((PAIRS, count, PAIR), BF),
        pltpu.VMEM((PAIRS, count, 2 * PAIR), BF),
    ]
    if last:
        scratch += [pltpu.VMEM(acc.shape, F32), pltpu.VMEM(ml.shape, F32)]
    wide = w_key.shape[0]
    return pl.pallas_call(
        functools.partial(attend_kernel, len(q_parts), len(pieces), first, last),
        out_shape=packed if last else (acc, ml),
        in_specs=[VMEM] * len(args),
        out_specs=VMEM if last else (VMEM, VMEM),
        scratch_shapes=scratch,
        cost_estimate=pl.CostEstimate(
            flops=16 * rows * count * wide + 4 * count * wide * wide,
            bytes_accessed=count * wide * 2 + rows * wide * 8,
            transcendentals=rows * count * HEADS,
        ),
        compiler_params=pltpu.CompilerParams(vmem_limit_bytes=56 * 1024 * 1024),
    )(*args)


def finish_kernel(parts, *refs):
    part_refs = refs[:parts]
    w_out, mlp_gain, w_hidden, w_back, w_flow, valid, flow = refs[parts:]
    rows = part_refs[0].shape[0]
    wide = PAIRS * PAIR
    levels = []
    for ref in part_refs:
        st = ref[:, wide:].astype(F32)
        levels.append(
            st[:, :HEADS] + st[:, HEADS:2 * HEADS] + st[:, 2 * HEADS:3 * HEADS]
        )
    best = functools.reduce(jnp.maximum, levels)
    shares = [jnp.exp(level - best) for level in levels]
    total = functools.reduce(jnp.add, shares)
    shares = [s / total for s in shares]
    half = lax.broadcasted_iota(jnp.int32, (rows, PAIR), 1) < DH
    projected = jnp.zeros((rows, w_out.shape[1]), F32)
    for p in range(PAIRS):
        mixed = jnp.zeros((rows, PAIR), F32)
        for ref, s in zip(part_refs, shares):
            weight = jnp.where(half, s[:, 2 * p:2 * p + 1], s[:, 2 * p + 1:2 * p + 2])
            mixed = mixed + weight * ref[:, p * PAIR:(p + 1) * PAIR].astype(F32)
        projected = projected + jnp.dot(
            mixed.astype(BF), w_out[p * PAIR:(p + 1) * PAIR, :], preferred_element_type=F32
        )
    z = layer_norm(projected, mlp_gain[...])
    pre = jnp.dot(z.astype(BF), w_hidden[...], preferred_element_type=F32)
    hidden = (0.5 * pre * (1.0 + lax.erf(pre * (0.5 ** 0.5)))).astype(BF)
    u = (z + jnp.dot(hidden, w_back[...], preferred_element_type=F32)).astype(BF)
    res = lax.dot_general(
        w_flow[...], u, (((1,), (1,)), ((), ())), preferred_element_type=F32
    )
    flow[...] = res * valid[...].astype(F32)


def local(
    queries,
    tile_ids,
    tile_table,
    valid,
    latents,
    lat_gain,
    query_gain,
    w_query,
    w_key,
    w_value,
    w_out,
    mlp_gain,
    w_hidden,
    w_back,
    w_flow,
):
    pb, lat = lax.axis_size("pb"), lax.axis_size("lat")
    both = ("pb", "lat")
    outer = math.gcd(pb, lat)
    inner = pb // outer
    group = inner * lat
    devices = pb * lat
    rows, depth = queries.shape
    share = rows // lat
    own_rows, wide = latents.shape
    tiles = tile_table.shape[0]

    def swap(value, stride):
        pairs = [(i, i ^ stride) for i in range(devices)]
        return lax.ppermute(value, both, pairs)

    def turn(value, k):
        pairs = [(i, (i + k * group) % devices) for i in range(devices)]
        return lax.ppermute(value, both, pairs)

    whole = lambda *shape: pl.BlockSpec(shape, lambda i, s: (0,) * len(shape))
    q_own, lat_own = pl.pallas_call(
        prepare_kernel,
        out_shape=(
            jax.ShapeDtypeStruct((share, w_query.shape[1]), BF),
            jax.ShapeDtypeStruct((own_rows, wide), BF),
        ),
        grid_spec=pltpu.PrefetchScalarGridSpec(
            num_scalar_prefetch=1,
            grid=(1,),
            in_specs=[
                pl.BlockSpec((share, depth), lambda i, s: (s[0], 0)),
                pl.BlockSpec((share, 1), lambda i, s: (s[0], 0)),
                whole(tiles, depth),
                whole(own_rows, wide),
                whole(1, wide),
                whole(1, depth),
                whole(*w_query.shape),
            ],
            out_specs=(whole(share, w_query.shape[1]), whole(own_rows, wide)),
        ),
    )(
        lax.axis_index("lat").reshape(1),
        queries,
        tile_ids.reshape(rows, 1),
        tile_table,
        latents,
        lat_gain.reshape(1, wide),
        query_gain.reshape(1, depth),
        w_query,
    )
    q_parts = [q_own] + [turn(q_own, k) for k in range(1, outer)]

    strides = [1 << i for i in range(1, group.bit_length() - 1)]
    assert 1 << (len(strides) + 1) == group
    halves = [lat_own[:own_rows // 2], lat_own[own_rows // 2:]]
    held = [[halves[0]], [halves[1]]]
    steps = [[lat_own, swap(lat_own, 1)]]
    orders = [strides, strides[::-1]]
    for j in range(len(strides)):
        arrived = []
        for c in range(2):
            stride = orders[c][j]
            if len(held[c]) > 2:
                held[c] = [jnp.concatenate(held[c])]
            new = [swap(piece, stride) for piece in held[c]]
            held[c] = held[c] + new
            arrived += new
        steps.append(arrived + [swap(piece, 1) for piece in arrived])
    state = None
    for j, pieces in enumerate(steps):
        state = attend(q_parts, pieces, w_key, w_value, state, j == len(steps) - 1)
    packed = state
    parts = [packed[:share]] + [
        turn(packed[k * share:(k + 1) * share], -k) for k in range(1, outer)
    ]
    args = [
        *parts, w_out, mlp_gain.reshape(1, depth), w_hidden, w_back, w_flow,
        valid.reshape(1, share),
    ]
    return pl.pallas_call(
        functools.partial(finish_kernel, outer),
        out_shape=jax.ShapeDtypeStruct((w_flow.shape[0], share), F32),
        in_specs=[VMEM] * len(args),
        out_specs=VMEM,
    )(*args)


def solution(mesh):
    placed = (
        P("pb", None),
        P("pb"),
        P(),
        P(("pb", "lat")),
        P(("pb", "lat"), None),
        P(),
        P(),
        P(),
        P(),
        P(),
        P(),
        P(),
        P(),
        P(),
        P(),
    )
    return jax.shard_map(
        local, mesh=mesh, in_specs=placed, out_specs=P(None, ("pb", "lat")), check_vma=False
    )
```

time: 362 us -> 108 us (0.30)
  matrix products: 106 us -> 0 us
  waiting for transfers between devices: 96.4 us -> 19.6 us
  other arithmetic: 66.8 us -> 0 us
  Pallas kernels: 0 us -> 55.8 us
  local copies, waits for them, and re-layouts: 65.4 us -> 11.5 us
  starting transfers between devices: 0.04 us -> 20.5 us
  between operations: 13.6 us -> 0.17 us
  blocking collectives: 10.7 us -> 0 us
    dot_general x39 -> x0, matrix products: 106 us -> none  [the longest x16 58.3 us: update(): jnp.einsum('hqd,khd->hqk', query_heads, key_part, preferred_element_type=...]
    all_gather x2 -> x0, waiting for transfers between devices: 96.4 us -> none  [the longest x1 73.8 us: local(): piece = lax.all_gather(lat_normed, 'pb', axis=0, tiled=True)]
    pallas_call x0 -> x5, Pallas kernels: none -> 55.8 us  [the longest x3 49 us: attend(): pl.pallas_call(functools.partial(attend_kernel, len(q_parts), len(pieces)...]
    reduce_sum x20 -> x0, other arithmetic: 51.6 us -> none  [the longest x16 48.8 us: update(): total = total * factor + jnp.sum(weights, axis=-1)]
    another operation x2 -> x0, local copies, waits for them, and re-layouts: 22.4 us -> none  [the longest x1 11.2 us: attend_rows(): key_blocks = keys.reshape(rows // step_rows, step_rows, heads, width)]
    ppermute x0 -> x19, starting transfers between devices: none -> 20.5 us  [the longest x6 10.5 us: turn(): return lax.ppermute(value, both, pairs)]
    ppermute x0 -> x19, waiting for transfers between devices: none -> 19.6 us  [the longest x6 19.5 us: turn(): return lax.ppermute(value, both, pairs)]
    unnamed x24 -> x44, local copies, waits for them, and re-layouts: 19.3 us -> 5.24 us
  transfers between devices with their start and end apart: 2 -> 19, of which waited for: 2 -> 4; matrix products, arithmetic and copies ran while one was open for 1% -> 2% of each run, Pallas kernels for 0% -> 24%
where the time goes in v1:
time: 108 us; the launch traced here: 107 us
  Pallas kernels  55.8 us (52%)
  starting transfers between devices  20.5 us (19%)
  waiting for transfers between devices  19.6 us (18%)
  local copies, waits for them, and re-layouts  11.5 us (11%)
    pallas_call x3, Pallas kernels, attend(): pl.pallas_call(functools.partial(attend_kernel, len(q_parts), len(pieces)...  49 us
    ppermute x6, waiting for transfers between devices, turn(): return lax.ppermute(value, both, pairs)  19.5 us
    ppermute x6, starting transfers between devices, turn(): return lax.ppermute(value, both, pairs)  10.5 us
    ppermute x13, starting transfers between devices, swap(): return lax.ppermute(value, both, pairs)  9.98 us
    unnamed x44, local copies, waits for them, and re-layouts  5.24 us
    pallas_call x1, Pallas kernels, local(): pl.pallas_call(functools.partial(finish_kernel, outer), out_shape=jax.Sha...  3.78 us
    pallas_call x1, Pallas kernels, local(): pl.pallas_call(prepare_kernel, out_shape=(jax.ShapeDtypeStruct((share, w_...  2.99 us
  transfers between devices with their start and end apart: 19, of which 4 were waited for; matrix products, arithmetic and copies ran while one was open for 2% of the time, Pallas kernels for 24%

profile of v1, /device:TPU:0, one launch (start us, length us, event | category | flops | bytes accessed | tf_op | source)
XLA Modules:
  0.0 107.5 jit_solution(13682054434500260432)
XLA Ops:
  0.0 1.9 %copy.18.queries = bf16[512,322]{1,0:T(8,128)(2,1)} copy(bf16[512,322]{0,1:T(8,128)(2,1)} %param.15) | data formatting | bytes 659456 | tf_op args[0]
  1.9 1.5 %copy.19.ids = s32[512,1]{1,0:T(8,128)} copy(s32[512,1]{0,1:T(1,128)} %bitcast.4) | data formatting | bytes 4096 | tf_op jit(solution)/shard_map/reshape | solution.py:260
  3.4 1.3 %reshape.21.query_gain = f32[1,322]{1,0:T(1,128)} reshape(f32[322]{0:T(512)} %param.21) | data formatting | bytes 2576 | tf_op jit(solution)/shard_map/reshape | solution.py:264
  4.7 3.0 %shard_map.145 = (bf16[128,512]{1,0:T(8,128)(2,1)}, bf16[512,512]{1,0:T(8,128)(2,1)}) custom-call(s32[1]{0:T(128)} %bitcast.part_ref, bf16[512,322]{1,0:T(8,128)(2,1)} %copy.18.queries, s32[512,1]{1,0:T(8,128)} %copy.19.ids, f32[64,322]{1,0:T(8,128)} %table.1, bf16[512,512]{1,0:T(8,128)(2,1)} %latents.1, f32[1,512]{1,0:T(1,128)} %bitcast.5, ...), custom_call_target="tpu_custom_call" | custom-call | tf_op jit(solution)/shard_map/pallas_call | solution.py:237
  7.7 0.5 collective-permute-start.15
  8.1 2.6 %collective-permute-start = (bf16[128,512]{1,0:T(8,128)(2,1)}, bf16[128,512]{1,0:T(8,128)(2,1)S(1)}, u32[]{:S(2)}, u32[]{:S(2)}) collective-permute-start(bf16[128,512]{1,0:T(8,128)(2,1)} %get-tuple-element.11.refs_0_), channel_id=1, source_target_pairs={{0,8},{1,9},{2,10},{3,11},{4,12},{5,13},{6,14},{7,15},{8,16},{9,17... | collective-permute-start | bytes 393224 | tf_op jit(solution)/shard_map/ppermute | solution.py:234
  10.7 2.6 %collective-permute-start.1 = (bf16[128,512]{1,0:T(8,128)(2,1)}, bf16[128,512]{1,0:T(8,128)(2,1)S(1)}, u32[]{:S(2)}, u32[]{:S(2)}) collective-permute-start(bf16[128,512]{1,0:T(8,128)(2,1)} %get-tuple-element.11.refs_0_), channel_id=1, source_target_pairs={{0,16},{1,17},{2,18},{3,19},{4,20},{5,21},{6,22},{7,23},{8,24},{9,... | collective-permute-start | bytes 393224 | tf_op jit(solution)/shard_map/ppermute | solution.py:234
  13.3 1.1 fusion.1
  14.4 1.6 %collective-permute-start.4 = (bf16[256,512]{1,0:T(8,128)(2,1)S(1)}, bf16[256,512]{1,0:T(8,128)(2,1)S(1)}, u32[]{:S(2)}, u32[]{:S(2)}) collective-permute-start(bf16[256,512]{1,0:T(8,128)(2,1)S(1)} %get-tuple-element.22), channel_id=1, source_target_pairs={{0,2},{1,3},{2,0},{3,1},{4,6},{5,7},{6,4},{7,5},{8,10},{9,11},{10,... | collective-permute-start | bytes 786440 | tf_op jit(solution)/shard_map/ppermute | solution.py:230
  15.9 1.5 %collective-permute-start.7 = (bf16[256,512]{1,0:T(8,128)(2,1)S(1)}, bf16[256,512]{1,0:T(8,128)(2,1)S(1)}, u32[]{:S(2)}, u32[]{:S(2)}) collective-permute-start(bf16[256,512]{1,0:T(8,128)(2,1)S(1)} %get-tuple-element.21), channel_id=1, source_target_pairs={{0,4},{1,5},{2,6},{3,7},{4,0},{5,1},{6,2},{7,3},{8,12},{9,13},{10,... | collective-permute-start | bytes 786440 | tf_op jit(solution)/shard_map/ppermute | solution.py:230
  17.4 0.0 collective-permute-done.refs_1_
  17.4 1.6 %collective-permute-start.6 = (bf16[256,512]{1,0:T(8,128)(2,1)S(1)}, bf16[256,512]{1,0:T(8,128)(2,1)S(1)}, u32[]{:S(2)}, u32[]{:S(2)}) collective-permute-start(bf16[256,512]{1,0:T(8,128)(2,1)S(1)} %get-tuple-element.21), channel_id=1, source_target_pairs={{0,2},{1,3},{2,0},{3,1},{4,6},{5,7},{6,4},{7,5},{8,10},{9,11},{10,... | collective-permute-start | bytes 786440 | tf_op jit(solution)/shard_map/ppermute | solution.py:230
  19.0 3.7 %collective-permute-done.1.refs_2_ = bf16[128,512]{1,0:T(8,128)(2,1)S(1)} collective-permute-done((bf16[128,512]{1,0:T(8,128)(2,1)}, bf16[128,512]{1,0:T(8,128)(2,1)S(1)}, u32[]{:S(2)}, u32[]{:S(2)}) %collective-permute-start.1) | collective-permute-done | bytes 131104 | tf_op jit(solution)/shard_map/ppermute | solution.py:234
  22.7 1.6 %collective-permute-start.2 = (bf16[128,512]{1,0:T(8,128)(2,1)}, bf16[128,512]{1,0:T(8,128)(2,1)S(1)}, u32[]{:S(2)}, u32[]{:S(2)}) collective-permute-start(bf16[128,512]{1,0:T(8,128)(2,1)} %get-tuple-element.11.refs_0_), channel_id=1, source_target_pairs={{0,24},{1,25},{2,26},{3,27},{4,28},{5,29},{6,30},{7,31},{8,0},{9,1... | collective-permute-start | bytes 393224 | tf_op jit(solution)/shard_map/ppermute | solution.py:234
  24.3 4.0 %collective-permute-done.2.refs_3_ = bf16[128,512]{1,0:T(8,128)(2,1)S(1)} collective-permute-done((bf16[128,512]{1,0:T(8,128)(2,1)}, bf16[128,512]{1,0:T(8,128)(2,1)S(1)}, u32[]{:S(2)}, u32[]{:S(2)}) %collective-permute-start.2) | collective-permute-done | bytes 131104 | tf_op jit(solution)/shard_map/ppermute | solution.py:234
  28.4 1.5 %collective-permute-start.3 = (bf16[256,512]{1,0:T(8,128)(2,1)S(1)}, bf16[256,512]{1,0:T(8,128)(2,1)S(1)}, u32[]{:S(2)}, u32[]{:S(2)}) collective-permute-start(bf16[256,512]{1,0:T(8,128)(2,1)S(1)} %get-tuple-element.22), channel_id=1, source_target_pairs={{0,4},{1,5},{2,6},{3,7},{4,0},{5,1},{6,2},{7,3},{8,12},{9,13},{10,... | collective-permute-start | bytes 786440 | tf_op jit(solution)/shard_map/ppermute | solution.py:230
  29.9 0.0 collective-permute-done.4.refs_4_
  29.9 0.0 collective-permute-start.13
  29.9 0.0 collective-permute-done.7.refs_5_
  29.9 0.0 copy-start.9
  29.9 0.6 collective-permute-start.5
  30.5 0.0 collective-permute-done.6.refs_6_
  30.5 0.2 collective-permute-start.14
  30.7 0.0 collective-permute-done.15.refs_5_
  30.7 1.5 %collective-permute-start.8 = (bf16[256,512]{1,0:T(8,128)(2,1)S(1)}, bf16[256,512]{1,0:T(8,128)(2,1)S(1)}, u32[]{:S(2)}, u32[]{:S(2)}) collective-permute-start(bf16[256,512]{1,0:T(8,128)(2,1)S(1)} %collective-permute-done.7.refs_5_), channel_id=1, source_target_pairs={{0,2},{1,3},{2,0},{3,1},{4,6},{5,7},{6,4},{7,5},{8,10},{9,11},{10,... | collective-permute-start | bytes 786440 | tf_op jit(solution)/shard_map/ppermute | solution.py:230
  32.2 0.0 copy-done.18
  32.2 0.0 copy-done.20
  32.2 11.9 %shard_map.146 = (f32[4,512,128]{2,1,0:T(8,128)}, f32[8,512,128]{2,1,0:T(8,128)}) custom-call(bf16[128,512]{1,0:T(8,128)(2,1)} %get-tuple-element.11.refs_0_, bf16[128,512]{1,0:T(8,128)(2,1)} %copy-done.18, bf16[128,512]{1,0:T(8,128)(2,1)} %copy-done.19, bf16[128,512]{1,0:T(8,128)(2,1)} %copy-done.20, bf16[512,512]{1,0:T(8,128)(2,1)} %get-tuple-element.12.refs_4_, ...), custom_call_target="tpu_custom_call" | custom-call | flops 5368709120 | bytes 3145728 | tf_op jit(solution)/shard_map/pallas_call | solution.py:150
  44.1 0.0 collective-permute-done.3.refs_4_
  44.1 0.1 collective-permute-start.11
  44.2 0.0 collective-permute-done.13.refs_6_
  44.2 0.4 collective-permute-start.9
  44.7 0.0 collective-permute-done.5.refs_5_
  44.7 0.1 collective-permute-start.10
  44.8 0.0 collective-permute-done.8.refs_7_
  44.8 0.4 collective-permute-start.12
  45.2 0.0 collective-permute-done.14.refs_7_
  45.2 0.7 copy-done.14
  46.0 13.6 %shard_map.147 = (f32[4,512,128]{2,1,0:T(8,128)}, f32[8,512,128]{2,1,0:T(8,128)}) custom-call(bf16[128,512]{1,0:T(8,128)(2,1)} %get-tuple-element.11.refs_0_, bf16[128,512]{1,0:T(8,128)(2,1)} %copy-done.18, bf16[128,512]{1,0:T(8,128)(2,1)} %copy-done.19, bf16[128,512]{1,0:T(8,128)(2,1)} %copy-done.20, bf16[256,512]{1,0:T(8,128)(2,1)} %copy-done.7, ...), custom_call_target="tpu_custom_call" | custom-call | flops 5368709120 | bytes 3145728 | tf_op jit(solution)/shard_map/pallas_call | solution.py:150
  59.5 0.0 copy-done.11
  59.6 0.0 collective-permute-done.11.refs_10_
  59.6 0.0 collective-permute-done.9.refs_8_
  59.6 0.0 collective-permute-done.10.refs_9_
  59.6 0.0 copy-start.16
  59.6 0.0 collective-permute-done.12.refs_11_
  59.6 0.6 copy-done.13
  60.3 0.1 copy-done.15
  60.4 0.1 copy-done.16
  60.5 0.1 copy-done.17
  60.6 23.6 %shard_map.148 = bf16[512,640]{1,0:T(8,128)(2,1)} custom-call(bf16[128,512]{1,0:T(8,128)(2,1)} %get-tuple-element.11.refs_0_, bf16[128,512]{1,0:T(8,128)(2,1)} %copy-done.18, bf16[128,512]{1,0:T(8,128)(2,1)} %copy-done.19, bf16[128,512]{1,0:T(8,128)(2,1)} %copy-done.20, bf16[256,512]{1,0:T(8,128)(2,1)} %copy-done.8, bf16[256,512]{1,0:T(8,128)(2,1)} %copy-done.10, ...), custom_call_target="tpu_custom_call" | custom-call | flops 10737418240 | bytes 4194304 | tf_op jit(solution)/shard_map/pallas_call | solution.py:150
  84.2 1.9 %fusion = (bf16[128,640]{1,0:T(8,128)(2,1)S(1)}, bf16[128,640]{1,0:T(8,128)(2,1)S(1)}, bf16[128,640]{1,0:T(8,128)(2,1)S(1)}, bf16[128,640]{1,0:T(8,128)(2,1)}) fusion(bf16[512,640]{1,0:T(8,128)(2,1)} %shard_map.148), kind=kLoop, calls=%fused_computation | loop fusion | bytes 1310720 | tf_op jit(solution)/shard_map/slice | solution.py:290
  86.0 3.1 %collective-permute-start.16 = (bf16[128,640]{1,0:T(8,128)(2,1)S(1)}, bf16[128,640]{1,0:T(8,128)(2,1)S(1)}, u32[]{:S(2)}, u32[]{:S(2)}) collective-permute-start(bf16[128,640]{1,0:T(8,128)(2,1)S(1)} %get-tuple-element.19), channel_id=1, source_target_pairs={{0,24},{1,25},{2,26},{3,27},{4,28},{5,29},{6,30},{7,31},{8,0},{9,1... | collective-permute-start | bytes 491528 | tf_op jit(solution)/shard_map/ppermute | solution.py:234
  89.1 0.0 collective-permute-start.17
  89.1 0.6 collective-permute-start.18
  89.7 0.0 copy-done
  89.7 0.9 copy.20.refs_4_
  90.6 0.5 reshape.22.refs_5_
  91.2 2.6 %collective-permute-done.16.refs_1_ = bf16[128,640]{1,0:T(8,128)(2,1)S(1)} collective-permute-done((bf16[128,640]{1,0:T(8,128)(2,1)S(1)}, bf16[128,640]{1,0:T(8,128)(2,1)S(1)}, u32[]{:S(2)}, u32[]{:S(2)}) %collective-permute-start.16) | collective-permute-done | bytes 163872 | tf_op jit(solution)/shard_map/ppermute | solution.py:234
  93.8 9.2 %collective-permute-done.17.refs_2_ = bf16[128,640]{1,0:T(8,128)(2,1)S(1)} collective-permute-done((bf16[128,640]{1,0:T(8,128)(2,1)S(1)}, bf16[128,640]{1,0:T(8,128)(2,1)S(1)}, u32[]{:S(2)}, u32[]{:S(2)}) %collective-permute-start.17) | collective-permute-done | bytes 163872 | tf_op jit(solution)/shard_map/ppermute | solution.py:234
  103.0 0.0 collective-permute-done.18.refs_3_
  103.0 0.0 copy-done.1
  103.0 0.7 copy-done.2
  103.6 0.1 copy-done.3
  103.7 3.8 %shard_map.149 = f32[2,128]{1,0:T(2,128)} custom-call(bf16[128,640]{1,0:T(8,128)(2,1)} %get-tuple-element.20.refs_0_, bf16[128,640]{1,0:T(8,128)(2,1)} %copy-done.1, bf16[128,640]{1,0:T(8,128)(2,1)} %copy-done.2, bf16[128,640]{1,0:T(8,128)(2,1)} %copy-done.3, bf16[512,322]{1,0:T(8,128)(2,1)} %copy.20.refs_4_, f32[1,322]{1,0:T(1,128)} %reshape.22.refs_5_, ...), custom_call_target="tpu_custom_call" | custom-call | tf_op jit(solution)/shard_map/pallas_call | solution.py:296
  (28 shorter events, 0.1 us)
Async XLA Ops:
  7.7 23.0 %collective-permute-start.15 = (bf16[512,512]{1,0:T(8,128)(2,1)}, bf16[512,512]{1,0:T(8,128)(2,1)S(1)}, u32[]{:S(2)}, u32[]{:S(2)}) collective-permute-start(bf16[512,512]{1,0:T(8,128)(2,1)} %get-tuple-element.12.refs_4_), channel_id=1, source_target_pairs={{0,1},{1,0},{2,3},{3,2},{4,5},{5,4},{6,7},{7,6},{8,9},{9,8},{10,11... | collective-permute-start | bytes 1572872 | tf_op jit(solution)/shard_map/ppermute | solution.py:230
  8.1 9.3 %collective-permute-start = (bf16[128,512]{1,0:T(8,128)(2,1)}, bf16[128,512]{1,0:T(8,128)(2,1)S(1)}, u32[]{:S(2)}, u32[]{:S(2)}) collective-permute-start(bf16[128,512]{1,0:T(8,128)(2,1)} %get-tuple-element.11.refs_0_), channel_id=1, source_target_pairs={{0,8},{1,9},{2,10},{3,11},{4,12},{5,13},{6,14},{7,15},{8,16},{9,17... | collective-permute-start | bytes 393224 | tf_op jit(solution)/shard_map/ppermute | solution.py:234
  10.7 12.0 %collective-permute-start.1 = (bf16[128,512]{1,0:T(8,128)(2,1)}, bf16[128,512]{1,0:T(8,128)(2,1)S(1)}, u32[]{:S(2)}, u32[]{:S(2)}) collective-permute-start(bf16[128,512]{1,0:T(8,128)(2,1)} %get-tuple-element.11.refs_0_), channel_id=1, source_target_pairs={{0,16},{1,17},{2,18},{3,19},{4,20},{5,21},{6,22},{7,23},{8,24},{9,... | collective-permute-start | bytes 393224 | tf_op jit(solution)/shard_map/ppermute | solution.py:234
  14.4 15.5 %collective-permute-start.4 = (bf16[256,512]{1,0:T(8,128)(2,1)S(1)}, bf16[256,512]{1,0:T(8,128)(2,1)S(1)}, u32[]{:S(2)}, u32[]{:S(2)}) collective-permute-start(bf16[256,512]{1,0:T(8,128)(2,1)S(1)} %get-tuple-element.22), channel_id=1, source_target_pairs={{0,2},{1,3},{2,0},{3,1},{4,6},{5,7},{6,4},{7,5},{8,10},{9,11},{10,... | collective-permute-start | bytes 786440 | tf_op jit(solution)/shard_map/ppermute | solution.py:230
  15.9 14.0 %collective-permute-start.7 = (bf16[256,512]{1,0:T(8,128)(2,1)S(1)}, bf16[256,512]{1,0:T(8,128)(2,1)S(1)}, u32[]{:S(2)}, u32[]{:S(2)}) collective-permute-start(bf16[256,512]{1,0:T(8,128)(2,1)S(1)} %get-tuple-element.21), channel_id=1, source_target_pairs={{0,4},{1,5},{2,6},{3,7},{4,0},{5,1},{6,2},{7,3},{8,12},{9,13},{10,... | collective-permute-start | bytes 786440 | tf_op jit(solution)/shard_map/ppermute | solution.py:230
  17.4 14.8 %copy-start.18 = (bf16[128,512]{1,0:T(8,128)(2,1)}, bf16[128,512]{1,0:T(8,128)(2,1)S(1)}, u32[]{:S(2)}) copy-start(bf16[128,512]{1,0:T(8,128)(2,1)S(1)} %collective-permute-done.refs_1_) | copy-start | bytes 393220
  17.4 13.1 %collective-permute-start.6 = (bf16[256,512]{1,0:T(8,128)(2,1)S(1)}, bf16[256,512]{1,0:T(8,128)(2,1)S(1)}, u32[]{:S(2)}, u32[]{:S(2)}) collective-permute-start(bf16[256,512]{1,0:T(8,128)(2,1)S(1)} %get-tuple-element.21), channel_id=1, source_target_pairs={{0,2},{1,3},{2,0},{3,1},{4,6},{5,7},{6,4},{7,5},{8,10},{9,11},{10,... | collective-permute-start | bytes 786440 | tf_op jit(solution)/shard_map/ppermute | solution.py:230
  22.7 9.5 %copy-start.19 = (bf16[128,512]{1,0:T(8,128)(2,1)}, bf16[128,512]{1,0:T(8,128)(2,1)S(1)}, u32[]{:S(2)}) copy-start(bf16[128,512]{1,0:T(8,128)(2,1)S(1)} %collective-permute-done.1.refs_2_) | copy-start | bytes 393220
  22.7 5.7 %collective-permute-start.2 = (bf16[128,512]{1,0:T(8,128)(2,1)}, bf16[128,512]{1,0:T(8,128)(2,1)S(1)}, u32[]{:S(2)}, u32[]{:S(2)}) collective-permute-start(bf16[128,512]{1,0:T(8,128)(2,1)} %get-tuple-element.11.refs_0_), channel_id=1, source_target_pairs={{0,24},{1,25},{2,26},{3,27},{4,28},{5,29},{6,30},{7,31},{8,0},{9,1... | collective-permute-start | bytes 393224 | tf_op jit(solution)/shard_map/ppermute | solution.py:234
  28.4 3.8 %copy-start.20 = (bf16[128,512]{1,0:T(8,128)(2,1)}, bf16[128,512]{1,0:T(8,128)(2,1)S(1)}, u32[]{:S(2)}) copy-start(bf16[128,512]{1,0:T(8,128)(2,1)S(1)} %collective-permute-done.2.refs_3_) | copy-start | bytes 393220
  28.4 15.7 %collective-permute-start.3 = (bf16[256,512]{1,0:T(8,128)(2,1)S(1)}, bf16[256,512]{1,0:T(8,128)(2,1)S(1)}, u32[]{:S(2)}, u32[]{:S(2)}) collective-permute-start(bf16[256,512]{1,0:T(8,128)(2,1)S(1)} %get-tuple-element.22), channel_id=1, source_target_pairs={{0,4},{1,5},{2,6},{3,7},{4,0},{5,1},{6,2},{7,3},{8,12},{9,13},{10,... | collective-permute-start | bytes 786440 | tf_op jit(solution)/shard_map/ppermute | solution.py:230
  29.9 14.2 %copy-start.7 = (bf16[256,512]{1,0:T(8,128)(2,1)}, bf16[256,512]{1,0:T(8,128)(2,1)S(1)}, u32[]{:S(2)}) copy-start(bf16[256,512]{1,0:T(8,128)(2,1)S(1)} %collective-permute-done.4.refs_4_) | copy-start | bytes 786436
  29.9 14.4 %collective-permute-start.13 = (bf16[256,512]{1,0:T(8,128)(2,1)S(1)}, bf16[256,512]{1,0:T(8,128)(2,1)S(1)}, u32[]{:S(2)}, u32[]{:S(2)}) collective-permute-start(bf16[256,512]{1,0:T(8,128)(2,1)S(1)} %collective-permute-done.4.refs_4_), channel_id=1, source_target_pairs={{0,1},{1,0},{2,3},{3,2},{4,5},{5,4},{6,7},{7,6},{8,9},{9,8},{10,11... | collective-permute-start | bytes 786440 | tf_op jit(solution)/shard_map/ppermute | solution.py:230
  29.9 14.2 %copy-start.9 = (bf16[256,512]{1,0:T(8,128)(2,1)}, bf16[256,512]{1,0:T(8,128)(2,1)S(1)}, u32[]{:S(2)}) copy-start(bf16[256,512]{1,0:T(8,128)(2,1)S(1)} %collective-permute-done.7.refs_5_) | copy-start | bytes 786436
  29.9 14.8 %collective-permute-start.5 = (bf16[256,512]{1,0:T(8,128)(2,1)S(1)}, bf16[256,512]{1,0:T(8,128)(2,1)S(1)}, u32[]{:S(2)}, u32[]{:S(2)}) collective-permute-start(bf16[256,512]{1,0:T(8,128)(2,1)S(1)} %collective-permute-done.4.refs_4_), channel_id=1, source_target_pairs={{0,4},{1,5},{2,6},{3,7},{4,0},{5,1},{6,2},{7,3},{8,12},{9,13},{10,... | collective-permute-start | bytes 786440 | tf_op jit(solution)/shard_map/ppermute | solution.py:230
  30.5 13.6 %copy-start.6 = (bf16[256,512]{1,0:T(8,128)(2,1)}, bf16[256,512]{1,0:T(8,128)(2,1)S(1)}, u32[]{:S(2)}) copy-start(bf16[256,512]{1,0:T(8,128)(2,1)S(1)} %collective-permute-done.6.refs_6_) | copy-start | bytes 786436
  30.5 14.7 %collective-permute-start.14 = (bf16[256,512]{1,0:T(8,128)(2,1)S(1)}, bf16[256,512]{1,0:T(8,128)(2,1)S(1)}, u32[]{:S(2)}, u32[]{:S(2)}) collective-permute-start(bf16[256,512]{1,0:T(8,128)(2,1)S(1)} %collective-permute-done.7.refs_5_), channel_id=1, source_target_pairs={{0,1},{1,0},{2,3},{3,2},{4,5},{5,4},{6,7},{7,6},{8,9},{9,8},{10,11... | collective-permute-start | bytes 786440 | tf_op jit(solution)/shard_map/ppermute | solution.py:230
  30.7 1.5 %copy-start.5 = (bf16[512,512]{1,0:T(8,128)(2,1)}, bf16[512,512]{1,0:T(8,128)(2,1)S(1)}, u32[]{:S(2)}) copy-start(bf16[512,512]{1,0:T(8,128)(2,1)S(1)} %collective-permute-done.15.refs_5_) | copy-start | bytes 1572868
  30.7 14.1 %collective-permute-start.8 = (bf16[256,512]{1,0:T(8,128)(2,1)S(1)}, bf16[256,512]{1,0:T(8,128)(2,1)S(1)}, u32[]{:S(2)}, u32[]{:S(2)}) collective-permute-start(bf16[256,512]{1,0:T(8,128)(2,1)S(1)} %collective-permute-done.7.refs_5_), channel_id=1, source_target_pairs={{0,2},{1,3},{2,0},{3,1},{4,6},{5,7},{6,4},{7,5},{8,10},{9,11},{10,... | collective-permute-start | bytes 786440 | tf_op jit(solution)/shard_map/ppermute | solution.py:230
  44.1 15.4 %copy-start.8 = (bf16[256,512]{1,0:T(8,128)(2,1)}, bf16[256,512]{1,0:T(8,128)(2,1)S(1)}, u32[]{:S(2)}) copy-start(bf16[256,512]{1,0:T(8,128)(2,1)S(1)} %collective-permute-done.3.refs_4_) | copy-start | bytes 786436
  44.1 15.5 %collective-permute-start.11 = (bf16[256,512]{1,0:T(8,128)(2,1)S(1)}, bf16[256,512]{1,0:T(8,128)(2,1)S(1)}, u32[]{:S(2)}, u32[]{:S(2)}) collective-permute-start(bf16[256,512]{1,0:T(8,128)(2,1)S(1)} %collective-permute-done.6.refs_6_), channel_id=1, source_target_pairs={{0,1},{1,0},{2,3},{3,2},{4,5},{5,4},{6,7},{7,6},{8,9},{9,8},{10,11... | collective-permute-start | bytes 786440 | tf_op jit(solution)/shard_map/ppermute | solution.py:230
  44.2 1.0 copy-start.12
  44.2 15.3 %collective-permute-start.9 = (bf16[256,512]{1,0:T(8,128)(2,1)S(1)}, bf16[256,512]{1,0:T(8,128)(2,1)S(1)}, u32[]{:S(2)}, u32[]{:S(2)}) collective-permute-start(bf16[256,512]{1,0:T(8,128)(2,1)S(1)} %collective-permute-done.3.refs_4_), channel_id=1, source_target_pairs={{0,1},{1,0},{2,3},{3,2},{4,5},{5,4},{6,7},{7,6},{8,9},{9,8},{10,11... | collective-permute-start | bytes 786440 | tf_op jit(solution)/shard_map/ppermute | solution.py:230
  44.7 14.9 %copy-start.10 = (bf16[256,512]{1,0:T(8,128)(2,1)}, bf16[256,512]{1,0:T(8,128)(2,1)S(1)}, u32[]{:S(2)}) copy-start(bf16[256,512]{1,0:T(8,128)(2,1)S(1)} %collective-permute-done.5.refs_5_) | copy-start | bytes 786436
  44.7 14.9 %collective-permute-start.10 = (bf16[256,512]{1,0:T(8,128)(2,1)S(1)}, bf16[256,512]{1,0:T(8,128)(2,1)S(1)}, u32[]{:S(2)}, u32[]{:S(2)}) collective-permute-start(bf16[256,512]{1,0:T(8,128)(2,1)S(1)} %collective-permute-done.5.refs_5_), channel_id=1, source_target_pairs={{0,1},{1,0},{2,3},{3,2},{4,5},{5,4},{6,7},{7,6},{8,9},{9,8},{10,11... | collective-permute-start | bytes 786440 | tf_op jit(solution)/shard_map/ppermute | solution.py:230
  44.8 14.8 %copy-start.11 = (bf16[256,512]{1,0:T(8,128)(2,1)}, bf16[256,512]{1,0:T(8,128)(2,1)S(1)}, u32[]{:S(2)}) copy-start(bf16[256,512]{1,0:T(8,128)(2,1)S(1)} %collective-permute-done.8.refs_7_) | copy-start | bytes 786436
  44.8 14.8 %collective-permute-start.12 = (bf16[256,512]{1,0:T(8,128)(2,1)S(1)}, bf16[256,512]{1,0:T(8,128)(2,1)S(1)}, u32[]{:S(2)}, u32[]{:S(2)}) collective-permute-start(bf16[256,512]{1,0:T(8,128)(2,1)S(1)} %collective-permute-done.8.refs_7_), channel_id=1, source_target_pairs={{0,1},{1,0},{2,3},{3,2},{4,5},{5,4},{6,7},{7,6},{8,9},{9,8},{10,11... | collective-permute-start | bytes 786440 | tf_op jit(solution)/shard_map/ppermute | solution.py:230
  45.2 0.7 copy-start.14
  59.6 0.7 copy-start.13
  59.6 0.8 copy-start.15
  59.6 0.9 copy-start.16
  59.6 0.9 copy-start.17
  60.6 29.2 %copy-start = (bf16[512,322]{0,1:T(8,128)(2,1)S(1)}, bf16[512,322]{0,1:T(8,128)(2,1)}, u32[]{:S(2)}) copy-start(bf16[512,322]{0,1:T(8,128)(2,1)} %param.25) | copy-start | bytes 989188
  60.6 30.1 %copy-start.4 = (f32[322]{0:T(512)S(1)}, f32[322]{0:T(512)}, u32[]{:S(2)}) copy-start(f32[322]{0:T(512)} %param.26) | copy-start | bytes 3868
  86.0 7.8 %collective-permute-start.16 = (bf16[128,640]{1,0:T(8,128)(2,1)S(1)}, bf16[128,640]{1,0:T(8,128)(2,1)S(1)}, u32[]{:S(2)}, u32[]{:S(2)}) collective-permute-start(bf16[128,640]{1,0:T(8,128)(2,1)S(1)} %get-tuple-element.19), channel_id=1, source_target_pairs={{0,24},{1,25},{2,26},{3,27},{4,28},{5,29},{6,30},{7,31},{8,0},{9,1... | collective-permute-start | bytes 491528 | tf_op jit(solution)/shard_map/ppermute | solution.py:234
  89.1 13.8 %collective-permute-start.17 = (bf16[128,640]{1,0:T(8,128)(2,1)S(1)}, bf16[128,640]{1,0:T(8,128)(2,1)S(1)}, u32[]{:S(2)}, u32[]{:S(2)}) collective-permute-start(bf16[128,640]{1,0:T(8,128)(2,1)S(1)} %get-tuple-element.18), channel_id=1, source_target_pairs={{0,16},{1,17},{2,18},{3,19},{4,20},{5,21},{6,22},{7,23},{8,24},{9,... | collective-permute-start | bytes 491528 | tf_op jit(solution)/shard_map/ppermute | solution.py:234
  89.1 13.8 %collective-permute-start.18 = (bf16[128,640]{1,0:T(8,128)(2,1)S(1)}, bf16[128,640]{1,0:T(8,128)(2,1)S(1)}, u32[]{:S(2)}, u32[]{:S(2)}) collective-permute-start(bf16[128,640]{1,0:T(8,128)(2,1)S(1)} %get-tuple-element.17), channel_id=1, source_target_pairs={{0,8},{1,9},{2,10},{3,11},{4,12},{5,13},{6,14},{7,15},{8,16},{9,17... | collective-permute-start | bytes 491528 | tf_op jit(solution)/shard_map/ppermute | solution.py:234
  93.8 9.2 %copy-start.1 = (bf16[128,640]{1,0:T(8,128)(2,1)}, bf16[128,640]{1,0:T(8,128)(2,1)S(1)}, u32[]{:S(2)}) copy-start(bf16[128,640]{1,0:T(8,128)(2,1)S(1)} %collective-permute-done.16.refs_1_) | copy-start | bytes 491524
  103.0 0.7 copy-start.2
  103.0 0.7 copy-start.3

commit v2 on v1

v2 whole, which is shorter than its diff:
```python
import functools
import math

import jax
import jax.numpy as jnp
from jax import lax
from jax.experimental import pallas as pl
from jax.experimental.pallas import tpu as pltpu
from jax.sharding import PartitionSpec as P

HEADS = 8
DH = 64
PAIR = 2 * DH
PAIRS = HEADS // 2
NEG = -1e30
BF = jnp.bfloat16
F32 = jnp.float32
MESH = pl.DeviceIdType.MESH
VMEM = pl.BlockSpec(memory_space=pltpu.VMEM)


def layer_norm(values, gain):
    center = values - jnp.mean(values, axis=-1, keepdims=True)
    spread = jnp.mean(center * center, axis=-1, keepdims=True)
    return center * lax.rsqrt(spread + 1e-05) * gain


def peers(outer, group):
    pb, lat = lax.axis_size("pb"), lax.axis_size("lat")
    me = lax.axis_index("pb") * lat + lax.axis_index("lat")
    devices = pb * lat

    def place(i):
        return (i // lat, i % lat)

    def ahead(k):
        return place((me + k * group + devices) % devices)

    def across(stride):
        return place(me + stride * (1 - 2 * ((me // stride) % 2)))

    return ahead, across


def greet(targets):
    barrier = pltpu.get_barrier_semaphore()
    for target in targets:
        pl.semaphore_signal(barrier, inc=1, device_id=target, device_id_type=MESH)
    pl.semaphore_wait(barrier, len(targets))


def prepare_kernel(
    outer, group, stride_a, stride_b, queries, ids, table, latents, lat_gain, query_gain, w_query,
    q_out, held_a, held_b, normed_a, normed_b, got_a, got_b, q_own, q_got, send_sem, recv_sem,
):
    ahead, across = peers(outer, group)
    greet([ahead(k) for k in range(1, outer)] + [across(stride_a), across(stride_b)])
    half = latents.shape[0] // 2
    copies = []
    for src, dst, stride, at in (
        (normed_a, got_a, stride_a, outer), (normed_b, got_b, stride_b, outer + 1)
    ):
        begin = (at - outer) * half
        src[...] = layer_norm(
            latents[begin:begin + half, :].astype(F32), lat_gain[...]
        ).astype(BF)
        copy = pltpu.make_async_remote_copy(
            src_ref=src, dst_ref=dst, send_sem=send_sem.at[at], recv_sem=recv_sem.at[at],
            device_id=across(stride), device_id_type=MESH,
        )
        copy.start()
        copies.append(copy)
    tiles = table.shape[0]
    share = q_own.shape[0]
    part = lax.axis_index("lat")
    lanes = lax.broadcasted_iota(jnp.int32, (tiles, share), 0)
    onehot = (ids[pl.ds(part, 1), :] == lanes).astype(F32)
    rows = queries[pl.ds(pl.multiple_of(part * share, share), share), :]
    shifted = rows.astype(F32) + lax.dot_general(
        onehot, table[...], (((0,), (0,)), ((), ())),
        precision=lax.Precision.HIGHEST, preferred_element_type=F32,
    )
    normed = layer_norm(shifted, query_gain[...]).astype(BF)
    q = jnp.dot(normed, w_query[...], preferred_element_type=F32).astype(BF)
    q = (q.astype(F32) * (DH ** -0.5)).astype(BF)
    q_own[...] = q
    for k in range(1, outer):
        copy = pltpu.make_async_remote_copy(
            src_ref=q_own, dst_ref=q_got.at[k], send_sem=send_sem.at[k], recv_sem=recv_sem.at[k],
            device_id=ahead(k), device_id_type=MESH,
        )
        copy.start()
        copies.append(copy)
    q_out[:share, :] = q
    held_a[:half, :] = normed_a[...]
    held_b[:half, :] = normed_b[...]
    for copy in copies:
        copy.wait()
    held_a[half:, :] = got_a[...]
    held_b[half:, :] = got_b[...]
    for k in range(1, outer):
        q_out[k * share:(k + 1) * share, :] = q_got[k]


def attend_kernel(pieces, first, last, *refs):
    refs = list(refs)
    q_ref = refs.pop(0)
    lat_refs = [refs.pop(0) for _ in range(pieces)]
    w_key, w_value = refs.pop(0), refs.pop(0)
    if not first:
        acc_in, stat_in = refs.pop(0), refs.pop(0)
    if last:
        out = refs.pop(0)
    else:
        acc_out, stat_out = refs.pop(0), refs.pop(0)
    keys, vals = refs
    rows = q_ref.shape[0]
    at = 0
    for ref in lat_refs:
        n = ref.shape[0]
        piece = ref[...]
        kk = jnp.dot(piece, w_key[...], preferred_element_type=F32)
        vv = jnp.dot(piece, w_value[...], preferred_element_type=F32).astype(BF)
        keys[:, at:at + n] = kk.T.astype(BF)
        for p in range(PAIRS):
            vals[p, at:at + n, :PAIR] = vv[:, p * PAIR:(p + 1) * PAIR]
            vals[p, at:at + n, PAIR:] = jnp.ones((n, PAIR), BF)
        at += n
    lane = lax.broadcasted_iota(jnp.int32, (rows, PAIR), 1)
    low = lane < DH

    def scores(g):
        p, h = g // 2, g % 2
        both = q_ref[:, p * PAIR:(p + 1) * PAIR]
        zero = jnp.zeros_like(both)
        mine = jnp.where(low, both, zero) if h == 0 else jnp.where(low, zero, both)
        return jnp.dot(mine, keys[p * PAIR:(p + 1) * PAIR, :], preferred_element_type=F32)

    stats = jnp.zeros((rows, PAIR), F32)
    ahead = scores(0)
    for g in range(HEADS):
        s = ahead
        if g + 1 < HEADS:
            ahead = scores(g + 1)
        p, h = g // 2, g % 2
        top = jnp.max(s, axis=-1, keepdims=True)
        if not first:
            old = stat_in[:, g:g + 1]
            top = jnp.maximum(top, old)
        w = jnp.exp((s - top).astype(BF))
        r = jnp.dot(w, vals[p], preferred_element_type=F32)
        total = r[:, PAIR:]
        mixed = r[:, :PAIR]
        if not first:
            factor = jnp.exp(old - top)
            total = total + factor * stat_in[:, HEADS + g:HEADS + g + 1]
            mixed = mixed + factor * acc_in[:, p * PAIR:(p + 1) * PAIR]
        if last:
            mixed = mixed / total
            level = top + jnp.log(total)
            hi = level.astype(BF).astype(F32)
            mid = (level - hi).astype(BF).astype(F32)
            stats = jnp.where(lane == g, hi, stats)
            stats = jnp.where(lane == HEADS + g, mid, stats)
            stats = jnp.where(lane == 2 * HEADS + g, level - hi - mid, stats)
        else:
            stats = jnp.where(lane == g, top, stats)
            stats = jnp.where(lane == HEADS + g, total, stats)
        if h == 0:
            kept = mixed
        else:
            new = jnp.where(low, kept, mixed)
            if last:
                out[:, p * PAIR:(p + 1) * PAIR] = new.astype(BF)
            else:
                acc_out[:, p * PAIR:(p + 1) * PAIR] = new
    if last:
        out[:, PAIRS * PAIR:] = stats.astype(BF)
    else:
        stat_out[...] = stats


def attend(q, pieces, w_key, w_value, state, last):
    first = state is None
    rows = q.shape[0]
    count = sum(p.shape[0] for p in pieces)
    acc = jax.ShapeDtypeStruct((rows, PAIRS * PAIR), F32)
    stats = jax.ShapeDtypeStruct((rows, PAIR), F32)
    packed = jax.ShapeDtypeStruct((rows, (PAIRS + 1) * PAIR), BF)
    args = [q, *pieces, w_key, w_value] + ([] if first else list(state))
    wide = w_key.shape[0]
    return pl.pallas_call(
        functools.partial(attend_kernel, len(pieces), first, last),
        out_shape=packed if last else (acc, stats),
        in_specs=[VMEM] * len(args),
        out_specs=VMEM if last else (VMEM, VMEM),
        scratch_shapes=[
            pltpu.VMEM((PAIRS * PAIR, count), BF),
            pltpu.VMEM((PAIRS, count, 2 * PAIR), BF),
        ],
        cost_estimate=pl.CostEstimate(
            flops=16 * rows * count * wide + 4 * count * wide * wide,
            bytes_accessed=count * wide * 2 + rows * wide * 8,
            transcendentals=rows * count * HEADS,
        ),
        compiler_params=pltpu.CompilerParams(vmem_limit_bytes=56 * 1024 * 1024),
    )(*args)


def finish_kernel(
    outer, group, packed, w_out, mlp_gain, w_hidden, w_back, w_flow, valid, flow,
    got, send_sem, recv_sem,
):
    ahead, across = peers(outer, group)
    greet([ahead(-k) for k in range(1, outer)])
    rows = got.shape[1]
    copies = []
    for k in range(1, outer):
        copy = pltpu.make_async_remote_copy(
            src_ref=packed.at[pl.ds(k * rows, rows)], dst_ref=got.at[k],
            send_sem=send_sem.at[k], recv_sem=recv_sem.at[k],
            device_id=ahead(-k), device_id_type=MESH,
        )
        copy.start()
        copies.append(copy)
    for copy in copies:
        copy.wait()
    part_refs = [packed.at[pl.ds(0, rows)]] + [got.at[k] for k in range(1, outer)]
    wide = PAIRS * PAIR
    levels = []
    for ref in part_refs:
        st = ref[:, wide:].astype(F32)
        levels.append(
            st[:, :HEADS] + st[:, HEADS:2 * HEADS] + st[:, 2 * HEADS:3 * HEADS]
        )
    best = functools.reduce(jnp.maximum, levels)
    shares = [jnp.exp(level - best) for level in levels]
    total = functools.reduce(jnp.add, shares)
    shares = [s / total for s in shares]
    half = lax.broadcasted_iota(jnp.int32, (rows, PAIR), 1) < DH
    projected = jnp.zeros((rows, w_out.shape[1]), F32)
    for p in range(PAIRS):
        mixed = jnp.zeros((rows, PAIR), F32)
        for ref, s in zip(part_refs, shares):
            weight = jnp.where(half, s[:, 2 * p:2 * p + 1], s[:, 2 * p + 1:2 * p + 2])
            mixed = mixed + weight * ref[:, p * PAIR:(p + 1) * PAIR].astype(F32)
        projected = projected + jnp.dot(
            mixed.astype(BF), w_out[p * PAIR:(p + 1) * PAIR, :], preferred_element_type=F32
        )
    z = layer_norm(projected, mlp_gain[...])
    pre = jnp.dot(z.astype(BF), w_hidden[...], preferred_element_type=F32)
    hidden = (0.5 * pre * (1.0 + lax.erf(pre * (0.5 ** 0.5)))).astype(BF)
    u = (z + jnp.dot(hidden, w_back[...], preferred_element_type=F32)).astype(BF)
    res = lax.dot_general(
        w_flow[...], u, (((1,), (1,)), ((), ())), preferred_element_type=F32
    )
    flow[...] = res * valid[...].astype(F32)


def local(
    queries,
    tile_ids,
    tile_table,
    valid,
    latents,
    lat_gain,
    query_gain,
    w_query,
    w_key,
    w_value,
    w_out,
    mlp_gain,
    w_hidden,
    w_back,
    w_flow,
):
    pb, lat = lax.axis_size("pb"), lax.axis_size("lat")
    both = ("pb", "lat")
    outer = math.gcd(pb, lat)
    inner = pb // outer
    group = inner * lat
    devices = pb * lat
    rows, depth = queries.shape
    share = rows // lat
    own_rows, wide = latents.shape
    tiles = tile_table.shape[0]

    def swap(value, stride):
        pairs = [(i, i ^ stride) for i in range(devices)]
        return lax.ppermute(value, both, pairs)

    strides = [1 << i for i in range(1, group.bit_length() - 1)]
    assert 1 << (len(strides) + 1) == group
    half = own_rows // 2
    da = w_query.shape[1]
    q, held_a, held_b = pl.pallas_call(
        functools.partial(prepare_kernel, outer, group, strides[0], strides[-1]),
        out_shape=(
            jax.ShapeDtypeStruct((outer * share, da), BF),
            jax.ShapeDtypeStruct((own_rows, wide), BF),
            jax.ShapeDtypeStruct((own_rows, wide), BF),
        ),
        in_specs=[VMEM] * 7,
        out_specs=(VMEM,) * 3,
        scratch_shapes=[pltpu.VMEM((half, wide), BF)] * 4 + [
            pltpu.VMEM((share, da), BF),
            pltpu.VMEM((outer, share, da), BF),
            pltpu.SemaphoreType.DMA((outer + 2,)),
            pltpu.SemaphoreType.DMA((outer + 2,)),
        ],
        compiler_params=pltpu.CompilerParams(
            collective_id=0, has_side_effects=True, vmem_limit_bytes=32 * 1024 * 1024
        ),
    )(
        queries,
        tile_ids.reshape(lat, share),
        tile_table,
        latents,
        lat_gain.reshape(1, wide),
        query_gain.reshape(1, depth),
        w_query,
    )
    held = [held_a, held_b]
    steps = [held, [swap(piece, 1) for piece in held]]
    orders = [strides, strides[::-1]]
    for j in range(1, len(strides)):
        arrived = [swap(held[c], orders[c][j]) for c in range(2)]
        steps.append(arrived + [swap(piece, 1) for piece in arrived])
        if j + 1 < len(strides):
            held = [jnp.concatenate([held[c], arrived[c]]) for c in range(2)]
    state = None
    for j, pieces in enumerate(steps):
        state = attend(q, pieces, w_key, w_value, state, j == len(steps) - 1)
    return pl.pallas_call(
        functools.partial(finish_kernel, outer, group),
        out_shape=jax.ShapeDtypeStruct((w_flow.shape[0], share), F32),
        in_specs=[VMEM] * 7,
        out_specs=VMEM,
        scratch_shapes=[
            pltpu.VMEM((outer, share, (PAIRS + 1) * PAIR), BF),
            pltpu.SemaphoreType.DMA((outer,)),
            pltpu.SemaphoreType.DMA((outer,)),
        ],
        compiler_params=pltpu.CompilerParams(
            collective_id=1, has_side_effects=True, vmem_limit_bytes=32 * 1024 * 1024
        ),
    )(
        state, w_out, mlp_gain.reshape(1, depth), w_hidden, w_back, w_flow,
        valid.reshape(1, share),
    )


def solution(mesh):
    placed = (
        P("pb", None),
        P("pb"),
        P(),
        P(("pb", "lat")),
        P(("pb", "lat"), None),
        P(),
        P(),
        P(),
        P(),
        P(),
        P(),
        P(),
        P(),
        P(),
        P(),
    )
    return jax.shard_map(
        local, mesh=mesh, in_specs=placed, out_specs=P(None, ("pb", "lat")), check_vma=False
    )
```

time: 108 us -> 96.8 us (0.90)
  Pallas kernels: 55.8 us -> 75.8 us
  starting transfers between devices: 20.5 us -> 2.5 us
  waiting for transfers between devices: 19.6 us -> 11.2 us
  local copies, waits for them, and re-layouts: 11.5 us -> 6.72 us
    pallas_call x5, Pallas kernels: 55.8 us -> 75.8 us  [the longest x3 37.1 us: attend(): pl.pallas_call(functools.partial(attend_kernel, len(pieces), first, last)...]
    ppermute x6 -> x0, waiting for transfers between devices: 19.5 us -> none  [turn(): return lax.ppermute(value, both, pairs)]
    ppermute x13 -> x6, waiting for transfers between devices: 0.03 us -> 11.2 us  [swap(): return lax.ppermute(value, both, pairs)]
    ppermute x6 -> x0, starting transfers between devices: 10.5 us -> none  [turn(): return lax.ppermute(value, both, pairs)]
    ppermute x13 -> x6, starting transfers between devices: 9.98 us -> 2.5 us  [swap(): return lax.ppermute(value, both, pairs)]
    slice x2 -> x0, local copies, waits for them, and re-layouts: 2.93 us -> none  [the longest x1 1.87 us: local(): packed[k * share:(k + 1) * share]]
    reshape x1 -> x0, local copies, waits for them, and re-layouts: 1.53 us -> none  [local(): tile_ids.reshape(rows, 1)]
    unnamed x44 -> x39, local copies, waits for them, and re-layouts: 5.24 us -> 6.72 us
  transfers between devices with their start and end apart: 19 -> 6, of which waited for: 4 -> 2; matrix products, arithmetic and copies ran while one was open for 2% -> 0% of each run, Pallas kernels for 24% -> 21%
where the time goes in v2:
time: 96.8 us; the launch traced here: 96.5 us
  Pallas kernels  75.8 us (78%)
  waiting for transfers between devices  11.2 us (12%)
  local copies, waits for them, and re-layouts  6.72 us (7%)
  starting transfers between devices  2.5 us (3%)
    pallas_call x3, Pallas kernels, attend(): pl.pallas_call(functools.partial(attend_kernel, len(pieces), first, last)...  37.1 us
    pallas_call x1, Pallas kernels, local(): pl.pallas_call(functools.partial(finish_kernel, outer, group), out_shape=...  21.7 us
    pallas_call x1, Pallas kernels, local(): pl.pallas_call(functools.partial(prepare_kernel, outer, group, strides[0]...  17 us
    ppermute x6, waiting for transfers between devices, swap(): return lax.ppermute(value, both, pairs)  11.2 us
    unnamed x39, local copies, waits for them, and re-layouts  6.72 us
    ppermute x6, starting transfers between devices, swap(): return lax.ppermute(value, both, pairs)  2.5 us
  transfers between devices with their start and end apart: 6, of which 2 were waited for; matrix products, arithmetic and copies ran while one was open for 0% of the time, Pallas kernels for 21%

profile of v2, /device:TPU:0, one launch (start us, length us, event | category | flops | bytes accessed | tf_op | source)
XLA Modules:
  0.0 96.5 jit_solution(7230273783556212201)
XLA Ops:
  0.0 0.0 copy-start.14
  0.0 0.0 copy-start.5
  0.0 0.0 copy-start.1
  0.0 1.2 %copy.16.queries = bf16[512,322]{1,0:T(8,128)(2,1)S(1)} copy(bf16[512,322]{0,1:T(8,128)(2,1)} %param.15) | data formatting | bytes 659456 | tf_op args[0]
  1.3 0.0 copy-done.14
  1.3 0.0 copy-start.7
  1.3 0.0 copy-start.6
  1.3 0.0 copy-done.5
  1.3 0.0 copy-done.1
  1.3 0.6 copy-done.7
  2.0 0.0 copy-done.6
  2.0 0.0 copy-start.2
  2.0 1.0 %copy-done.2 = bf16[322,512]{1,0:T(8,128)(2,1)S(1)} copy-done((bf16[322,512]{1,0:T(8,128)(2,1)S(1)}, bf16[322,512]{1,0:T(8,128)(2,1)}, u32[]{:S(2)}) %copy-start.2) | copy-done | bytes 329752
  3.0 17.0 %shard_map.145 = (bf16[512,512]{1,0:T(8,128)(2,1)S(1)}, bf16[512,512]{1,0:T(8,128)(2,1)S(1)}, bf16[512,512]{1,0:T(8,128)(2,1)S(1)}) custom-call(bf16[512,322]{1,0:T(8,128)(2,1)S(1)} %copy.16.queries, s32[4,128]{1,0:T(4,128)S(1)} %bitcast.3, f32[64,322]{1,0:T(8,128)S(1)} %copy-done.5, bf16[512,512]{1,0:T(8,128)(2,1)S(1)} %copy-done.1, f32[1,512]{1,0:T(1,128)S(1)} %bitcast.4, ...), custom_call_target="tpu_custom_call" | custom-call | tf_op jit(solution)/shard_map/pallas_call | solution.py:296
  20.0 0.0 copy-start.10
  20.0 0.8 copy-done.10
  20.8 0.0 copy-start.11
  20.8 0.0 copy-start.12
  20.8 1.5 %collective-permute-start = (bf16[512,512]{1,0:T(8,128)(2,1)S(1)}, bf16[512,512]{1,0:T(8,128)(2,1)S(1)}, u32[]{:S(2)}, u32[]{:S(2)}) collective-permute-start(bf16[512,512]{1,0:T(8,128)(2,1)S(1)} %get-tuple-element.13.refs_1_), channel_id=1, source_target_pairs={{0,4},{1,5},{2,6},{3,7},{4,0},{5,1},{6,2},{7,3},{8,12},{9,13},{10,... | collective-permute-start | bytes 1572872 | tf_op jit(solution)/shard_map/ppermute | solution.py:290
  22.3 0.5 collective-permute-start.1
  22.8 0.0 collective-permute-start.4
  22.8 0.5 collective-permute-start.5
  23.3 9.2 %collective-permute-done.refs_1_ = bf16[512,512]{1,0:T(8,128)(2,1)S(1)} collective-permute-done((bf16[512,512]{1,0:T(8,128)(2,1)S(1)}, bf16[512,512]{1,0:T(8,128)(2,1)S(1)}, u32[]{:S(2)}, u32[]{:S(2)}) %collective-permute-start) | collective-permute-done | bytes 524320 | tf_op jit(solution)/shard_map/ppermute | solution.py:290
  32.5 0.0 copy-start.16
  32.5 0.0 collective-permute-start.2
  32.5 2.0 %collective-permute-done.1.refs_2_ = bf16[512,512]{1,0:T(8,128)(2,1)S(1)} collective-permute-done((bf16[512,512]{1,0:T(8,128)(2,1)S(1)}, bf16[512,512]{1,0:T(8,128)(2,1)S(1)}, u32[]{:S(2)}, u32[]{:S(2)}) %collective-permute-start.1) | collective-permute-done | bytes 524320 | tf_op jit(solution)/shard_map/ppermute | solution.py:290
  34.5 0.0 copy-start.17
  34.5 0.0 collective-permute-start.3
  34.5 0.0 copy-done.11
  34.5 0.0 copy-done.12
  34.5 0.0 copy-start.13
  34.5 9.1 %shard_map.146 = (f32[512,512]{1,0:T(8,128)}, f32[512,128]{1,0:T(8,128)}) custom-call(bf16[512,512]{1,0:T(8,128)(2,1)} %copy-done.10, bf16[512,512]{1,0:T(8,128)(2,1)} %copy-done.12, bf16[512,512]{1,0:T(8,128)(2,1)} %copy-done.11, bf16[512,512]{1,0:T(8,128)(2,1)} %refs_5_.1, bf16[512,512]{1,0:T(8,128)(2,1)} %refs_6_.1), custom_call_target="tpu_custom_call" | custom-call | flops 5368709120 | bytes 3145728 | tf_op jit(solution)/shard_map/pallas_call | solution.py:192
  43.6 0.0 copy-done.16
  43.6 0.0 copy-done.17
  43.6 0.0 copy-done.13
  43.6 0.0 copy-start.15
  43.6 0.2 copy.17.w_out
  43.9 0.5 copy-done.15
  44.3 0.0 collective-permute-done.4.refs_1_
  44.3 0.0 collective-permute-done.5.refs_2_
  44.3 11.0 %shard_map.147 = (f32[512,512]{1,0:T(8,128)}, f32[512,128]{1,0:T(8,128)}) custom-call(bf16[512,512]{1,0:T(8,128)(2,1)} %copy-done.10, bf16[512,512]{1,0:T(8,128)(2,1)} %collective-permute-done.4.refs_1_, bf16[512,512]{1,0:T(8,128)(2,1)} %collective-permute-done.5.refs_2_, bf16[512,512]{1,0:T(8,128)(2,1)} %refs_5_.1, bf16[512,512]{1,0:T(8,128)(2,1)} %refs_6_.1, ...), custom_call_target="tpu_custom_call" | custom-call | flops 5368709120 | bytes 3145728 | tf_op jit(solution)/shard_map/pallas_call | solution.py:192
  55.3 0.0 collective-permute-done.2.refs_3_
  55.3 0.0 collective-permute-done.3.refs_4_
  55.3 0.0 copy-start.3
  55.3 0.0 copy-start.4
  55.4 0.0 copy-start.9
  55.4 17.1 %shard_map.148.packed = bf16[512,640]{1,0:T(8,128)(2,1)} custom-call(bf16[512,512]{1,0:T(8,128)(2,1)} %copy-done.10, bf16[512,512]{1,0:T(8,128)(2,1)} %copy-done.16, bf16[512,512]{1,0:T(8,128)(2,1)} %copy-done.17, bf16[512,512]{1,0:T(8,128)(2,1)} %collective-permute-done.2.refs_3_, bf16[512,512]{1,0:T(8,128)(2,1)} %collective-permute-done.3.refs_4_, ...), custom_call_target="tpu_custom_call" | custom-call | flops 10737418240 | bytes 4194304 | tf_op jit(solution)/shard_map/pallas_call | solution.py:192
  72.4 0.0 copy-start.8
  72.4 0.0 copy-done.3
  72.4 0.0 copy-done.4
  72.4 0.0 copy-done.9
  72.5 0.7 copy-done.8
  73.1 0.0 copy-start
  73.1 1.1 %copy-done = bf16[512,640]{1,0:T(8,128)(2,1)S(1)} copy-done((bf16[512,640]{1,0:T(8,128)(2,1)S(1)}, bf16[512,640]{1,0:T(8,128)(2,1)}, u32[]{:S(2)}) %copy-start) | copy-done | bytes 655384
  74.2 21.7 %shard_map.149 = f32[2,128]{1,0:T(2,128)S(1)} custom-call(bf16[512,640]{1,0:T(8,128)(2,1)S(1)} %copy-done, bf16[512,322]{1,0:T(8,128)(2,1)S(1)} %copy.17.w_out, f32[1,322]{1,0:T(1,128)S(1)} %reshape.18.mlp_gain, bf16[322,322]{1,0:T(8,128)(2,1)S(1)} %copy-done.3, bf16[322,322]{1,0:T(8,128)(2,1)S(1)} %copy-done.4, bf16[2,322]{1,0:T(2,128)(2,1)S(1)} %copy-done.8, ...), custom_call_target="tpu_custom_call" | custom-call | tf_op jit(solution)/shard_map/pallas_call | solution.py:334
  95.9 0.6 copy.19
  (2 shorter events, 0.0 us)
Async XLA Ops:
  0.0 1.3 %copy-start.14 = (f32[322]{0:T(512)S(1)}, f32[322]{0:T(512)}, u32[]{:S(2)}) copy-start(f32[322]{0:T(512)} %param.21) | copy-start | bytes 3868
  0.0 1.3 %copy-start.5 = (f32[64,322]{1,0:T(8,128)S(1)}, f32[64,322]{1,0:T(8,128)}, u32[]{:S(2)}) copy-start(f32[64,322]{1,0:T(8,128)} %table.1) | copy-start | bytes 247300
  0.0 1.3 %copy-start.1 = (bf16[512,512]{1,0:T(8,128)(2,1)S(1)}, bf16[512,512]{1,0:T(8,128)(2,1)}, u32[]{:S(2)}) copy-start(bf16[512,512]{1,0:T(8,128)(2,1)} %latents.1) | copy-start | bytes 1572868
  1.3 0.7 copy-start.7
  1.3 0.7 copy-start.6
  2.0 1.0 %copy-start.2 = (bf16[322,512]{1,0:T(8,128)(2,1)S(1)}, bf16[322,512]{1,0:T(8,128)(2,1)}, u32[]{:S(2)}) copy-start(bf16[322,512]{1,0:T(8,128)(2,1)} %w_query.1) | copy-start | bytes 989188
  20.0 0.8 copy-start.10
  20.8 13.7 %copy-start.11 = (bf16[512,512]{1,0:T(8,128)(2,1)}, bf16[512,512]{1,0:T(8,128)(2,1)S(1)}, u32[]{:S(2)}) copy-start(bf16[512,512]{1,0:T(8,128)(2,1)S(1)} %get-tuple-element.14.refs_2_) | copy-start | bytes 1572868
  20.8 13.7 %copy-start.12 = (bf16[512,512]{1,0:T(8,128)(2,1)}, bf16[512,512]{1,0:T(8,128)(2,1)S(1)}, u32[]{:S(2)}) copy-start(bf16[512,512]{1,0:T(8,128)(2,1)S(1)} %get-tuple-element.13.refs_1_) | copy-start | bytes 1572868
  20.8 11.7 %collective-permute-start = (bf16[512,512]{1,0:T(8,128)(2,1)S(1)}, bf16[512,512]{1,0:T(8,128)(2,1)S(1)}, u32[]{:S(2)}, u32[]{:S(2)}) collective-permute-start(bf16[512,512]{1,0:T(8,128)(2,1)S(1)} %get-tuple-element.13.refs_1_), channel_id=1, source_target_pairs={{0,4},{1,5},{2,6},{3,7},{4,0},{5,1},{6,2},{7,3},{8,12},{9,13},{10,... | collective-permute-start | bytes 1572872 | tf_op jit(solution)/shard_map/ppermute | solution.py:290
  22.3 12.2 %collective-permute-start.1 = (bf16[512,512]{1,0:T(8,128)(2,1)S(1)}, bf16[512,512]{1,0:T(8,128)(2,1)S(1)}, u32[]{:S(2)}, u32[]{:S(2)}) collective-permute-start(bf16[512,512]{1,0:T(8,128)(2,1)S(1)} %get-tuple-element.14.refs_2_), channel_id=1, source_target_pairs={{0,2},{1,3},{2,0},{3,1},{4,6},{5,7},{6,4},{7,5},{8,10},{9,11},{10,... | collective-permute-start | bytes 1572872 | tf_op jit(solution)/shard_map/ppermute | solution.py:290
  22.8 21.5 %collective-permute-start.4 = (bf16[512,512]{1,0:T(8,128)(2,1)S(1)}, bf16[512,512]{1,0:T(8,128)(2,1)}, u32[]{:S(2)}, u32[]{:S(2)}) collective-permute-start(bf16[512,512]{1,0:T(8,128)(2,1)S(1)} %get-tuple-element.13.refs_1_), channel_id=1, source_target_pairs={{0,1},{1,0},{2,3},{3,2},{4,5},{5,4},{6,7},{7,6},{8,9},{9,8},{10,11... | collective-permute-start | bytes 1572872 | tf_op jit(solution)/shard_map/ppermute | solution.py:290
  22.8 21.5 %collective-permute-start.5 = (bf16[512,512]{1,0:T(8,128)(2,1)S(1)}, bf16[512,512]{1,0:T(8,128)(2,1)}, u32[]{:S(2)}, u32[]{:S(2)}) collective-permute-start(bf16[512,512]{1,0:T(8,128)(2,1)S(1)} %get-tuple-element.14.refs_2_), channel_id=1, source_target_pairs={{0,1},{1,0},{2,3},{3,2},{4,5},{5,4},{6,7},{7,6},{8,9},{9,8},{10,11... | collective-permute-start | bytes 1572872 | tf_op jit(solution)/shard_map/ppermute | solution.py:290
  32.5 11.1 %copy-start.16 = (bf16[512,512]{1,0:T(8,128)(2,1)}, bf16[512,512]{1,0:T(8,128)(2,1)S(1)}, u32[]{:S(2)}) copy-start(bf16[512,512]{1,0:T(8,128)(2,1)S(1)} %collective-permute-done.refs_1_) | copy-start | bytes 1572868
  32.5 22.8 %collective-permute-start.2 = (bf16[512,512]{1,0:T(8,128)(2,1)S(1)}, bf16[512,512]{1,0:T(8,128)(2,1)}, u32[]{:S(2)}, u32[]{:S(2)}) collective-permute-start(bf16[512,512]{1,0:T(8,128)(2,1)S(1)} %collective-permute-done.refs_1_), channel_id=1, source_target_pairs={{0,1},{1,0},{2,3},{3,2},{4,5},{5,4},{6,7},{7,6},{8,9},{9,8},{10,11... | collective-permute-start | bytes 1572872 | tf_op jit(solution)/shard_map/ppermute | solution.py:290
  34.5 9.1 %copy-start.17 = (bf16[512,512]{1,0:T(8,128)(2,1)}, bf16[512,512]{1,0:T(8,128)(2,1)S(1)}, u32[]{:S(2)}) copy-start(bf16[512,512]{1,0:T(8,128)(2,1)S(1)} %collective-permute-done.1.refs_2_) | copy-start | bytes 1572868
  34.5 20.8 %collective-permute-start.3 = (bf16[512,512]{1,0:T(8,128)(2,1)S(1)}, bf16[512,512]{1,0:T(8,128)(2,1)}, u32[]{:S(2)}, u32[]{:S(2)}) collective-permute-start(bf16[512,512]{1,0:T(8,128)(2,1)S(1)} %collective-permute-done.1.refs_2_), channel_id=1, source_target_pairs={{0,1},{1,0},{2,3},{3,2},{4,5},{5,4},{6,7},{7,6},{8,9},{9,8},{10,11... | collective-permute-start | bytes 1572872 | tf_op jit(solution)/shard_map/ppermute | solution.py:290
  34.5 9.1 %copy-start.13 = (bf16[512,322]{0,1:T(8,128)(2,1)S(1)}, bf16[512,322]{0,1:T(8,128)(2,1)}, u32[]{:S(2)}) copy-start(bf16[512,322]{0,1:T(8,128)(2,1)} %param.25) | copy-start | bytes 989188
  43.6 0.7 copy-start.15
  55.3 17.1 %copy-start.3 = (bf16[322,322]{1,0:T(8,128)(2,1)S(1)}, bf16[322,322]{1,0:T(8,128)(2,1)}, u32[]{:S(2)}) copy-start(bf16[322,322]{1,0:T(8,128)(2,1)} %w_hidden.1) | copy-start | bytes 622108
  55.3 17.1 %copy-start.4 = (bf16[322,322]{1,0:T(8,128)(2,1)S(1)}, bf16[322,322]{1,0:T(8,128)(2,1)}, u32[]{:S(2)}) copy-start(bf16[322,322]{1,0:T(8,128)(2,1)} %w_back.1) | copy-start | bytes 622108
  55.4 17.1 %copy-start.9 = (s32[128]{0:T(128)S(1)}, s32[128]{0:T(128)}, u32[]{:S(2)}) copy-start(s32[128]{0:T(128)} %param.18) | copy-start | bytes 1540
  72.4 0.7 copy-start.8
  73.1 1.1 %copy-start = (bf16[512,640]{1,0:T(8,128)(2,1)S(1)}, bf16[512,640]{1,0:T(8,128)(2,1)}, u32[]{:S(2)}) copy-start(bf16[512,640]{1,0:T(8,128)(2,1)} %shard_map.148.packed) | copy-start | bytes 1966084

commit v3 on v2

--- a/solution.py
+++ b/solution.py
@@ -55,8 +55,29 @@
 ):
     ahead, across = peers(outer, group)
     greet([ahead(k) for k in range(1, outer)] + [across(stride_a), across(stride_b)])
+    copies = []
+    tiles = table.shape[0]
+    share = q_own.shape[0]
+    part = lax.axis_index("lat")
+    lanes = lax.broadcasted_iota(jnp.int32, (tiles, share), 0)
+    onehot = (ids[pl.ds(part, 1), :] == lanes).astype(F32)
+    rows = queries[pl.ds(pl.multiple_of(part * share, share), share), :]
+    shifted = rows.astype(F32) + lax.dot_general(
+        onehot, table[...], (((0,), (0,)), ((), ())),
+        precision=lax.Precision.HIGHEST, preferred_element_type=F32,
+    )
+    normed = layer_norm(shifted, query_gain[...]).astype(BF)
+    q = jnp.dot(normed, w_query[...], preferred_element_type=F32).astype(BF)
+    q = (q.astype(F32) * (DH ** -0.5)).astype(BF)
+    q_own[...] = q
+    for k in range(1, outer):
+        copy = pltpu.make_async_remote_copy(
+            src_ref=q_own, dst_ref=q_got.at[k], send_sem=send_sem.at[k], recv_sem=recv_sem.at[k],
+            device_id=ahead(k), device_id_type=MESH,
+        )
+        copy.start()
+        copies.append(copy)
     half = latents.shape[0] // 2
-    copies = []
     for src, dst, stride, at in (
         (normed_a, got_a, stride_a, outer), (normed_b, got_b, stride_b, outer + 1)
     ):
@@ -67,27 +88,6 @@
         copy = pltpu.make_async_remote_copy(
             src_ref=src, dst_ref=dst, send_sem=send_sem.at[at], recv_sem=recv_sem.at[at],
             device_id=across(stride), device_id_type=MESH,
-        )
-        copy.start()
-        copies.append(copy)
-    tiles = table.shape[0]
-    share = q_own.shape[0]
-    part = lax.axis_index("lat")
-    lanes = lax.broadcasted_iota(jnp.int32, (tiles, share), 0)
-    onehot = (ids[pl.ds(part, 1), :] == lanes).astype(F32)
-    rows = queries[pl.ds(pl.multiple_of(part * share, share), share), :]
-    shifted = rows.astype(F32) + lax.dot_general(
-        onehot, table[...], (((0,), (0,)), ((), ())),
-        precision=lax.Precision.HIGHEST, preferred_element_type=F32,
-    )
-    normed = layer_norm(shifted, query_gain[...]).astype(BF)
-    q = jnp.dot(normed, w_query[...], preferred_element_type=F32).astype(BF)
-    q = (q.astype(F32) * (DH ** -0.5)).astype(BF)
-    q_own[...] = q
-    for k in range(1, outer):
-        copy = pltpu.make_async_remote_copy(
-            src_ref=q_own, dst_ref=q_got.at[k], send_sem=send_sem.at[k], recv_sem=recv_sem.at[k],
-            device_id=ahead(k), device_id_type=MESH,
         )
         copy.start()
         copies.append(copy)
@@ -321,16 +321,21 @@
         w_query,
     )
     held = [held_a, held_b]
-    steps = [held, [swap(piece, 1) for piece in held]]
     orders = [strides, strides[::-1]]
+    near = [swap(piece, 1) for piece in held]
+    far = [swap(held[c], orders[c][1 % len(strides)]) for c in range(2)]
+    state = attend(q, held, w_key, w_value, None, False)
+    pending = near
     for j in range(1, len(strides)):
-        arrived = [swap(held[c], orders[c][j]) for c in range(2)]
-        steps.append(arrived + [swap(piece, 1) for piece in arrived])
+        far, state = lax.optimization_barrier((far, state))
+        arrived = far
+        near = [swap(piece, 1) for piece in arrived]
         if j + 1 < len(strides):
             held = [jnp.concatenate([held[c], arrived[c]]) for c in range(2)]
-    state = None
-    for j, pieces in enumerate(steps):
-        state = attend(q, pieces, w_key, w_value, state, j == len(steps) - 1)
+            far = [swap(held[c], orders[c][j + 1]) for c in range(2)]
+        state = attend(q, pending, w_key, w_value, state, False)
+        pending = arrived + near
+    state = attend(q, pending, w_key, w_value, state, True)
     return pl.pallas_call(
         functools.partial(finish_kernel, outer, group),
         out_shape=jax.ShapeDtypeStruct((w_flow.shape[0], share), F32),

time: 96.8 us -> 86.9 us (0.90)
  waiting for transfers between devices: 11.2 us -> 2.23 us
    ppermute x6, waiting for transfers between devices: 11.2 us -> 2.23 us  [swap(): return lax.ppermute(value, both, pairs)]
  transfers between devices with their start and end apart: 6 -> 6, of which waited for: 2 -> 2; matrix products, arithmetic and copies ran while one was open for 0% -> 0% of each run, Pallas kernels for 21% -> 23%
where the time goes in v3:
time: 86.9 us; the launch traced here: 86.6 us
  Pallas kernels  74.9 us (86%)
  local copies, waits for them, and re-layouts  6.27 us (7%)
  starting transfers between devices  3.01 us (3%)
  waiting for transfers between devices  2.23 us (3%)
    pallas_call x3, Pallas kernels, attend(): pl.pallas_call(functools.partial(attend_kernel, len(pieces), first, last)...  37 us
    pallas_call x1, Pallas kernels, local(): pl.pallas_call(functools.partial(finish_kernel, outer, group), out_shape=...  21.4 us
    pallas_call x1, Pallas kernels, local(): pl.pallas_call(functools.partial(prepare_kernel, outer, group, strides[0]...  16.5 us
    unnamed x39, local copies, waits for them, and re-layouts  6.26 us
    ppermute x6, starting transfers between devices, swap(): return lax.ppermute(value, both, pairs)  3.01 us
    ppermute x6, waiting for transfers between devices, swap(): return lax.ppermute(value, both, pairs)  2.23 us
  transfers between devices with their start and end apart: 6, of which 2 were waited for; matrix products, arithmetic and copies ran while one was open for 0% of the time, Pallas kernels for 23%

profile of v3, /device:TPU:0, one launch (start us, length us, event | category | flops | bytes accessed | tf_op | source)
XLA Modules:
  0.0 86.6 jit_solution(17319369230066431372)
XLA Ops:
  0.0 0.0 copy-start.14
  0.0 0.0 copy-start.5
  0.0 0.0 copy-start.1
  0.0 1.2 %copy.16.queries = bf16[512,322]{1,0:T(8,128)(2,1)S(1)} copy(bf16[512,322]{0,1:T(8,128)(2,1)} %param.15) | data formatting | bytes 659456 | tf_op args[0]
  1.3 0.0 copy-done.14
  1.3 0.0 copy-start.7
  1.3 0.0 copy-start.6
  1.3 0.0 copy-done.5
  1.3 0.0 copy-done.1
  1.3 0.6 copy-done.7
  2.0 0.0 copy-done.6
  2.0 0.0 copy-start.2
  2.0 1.0 %copy-done.2 = bf16[322,512]{1,0:T(8,128)(2,1)S(1)} copy-done((bf16[322,512]{1,0:T(8,128)(2,1)S(1)}, bf16[322,512]{1,0:T(8,128)(2,1)}, u32[]{:S(2)}) %copy-start.2) | copy-done | bytes 329752
  3.0 16.5 %shard_map.145 = (bf16[512,512]{1,0:T(8,128)(2,1)S(1)}, bf16[512,512]{1,0:T(8,128)(2,1)S(1)}, bf16[512,512]{1,0:T(8,128)(2,1)S(1)}) custom-call(bf16[512,322]{1,0:T(8,128)(2,1)S(1)} %copy.16.queries, s32[4,128]{1,0:T(4,128)S(1)} %bitcast.3, f32[64,322]{1,0:T(8,128)S(1)} %copy-done.5, bf16[512,512]{1,0:T(8,128)(2,1)S(1)} %copy-done.1, f32[1,512]{1,0:T(1,128)S(1)} %bitcast.4, ...), custom_call_target="tpu_custom_call" | custom-call | tf_op jit(solution)/shard_map/pallas_call | solution.py:296
  19.5 0.0 copy-start.10
  19.5 0.8 copy-done.10
  20.3 0.0 copy-start.11
  20.3 0.0 copy-start.12
  20.3 1.5 %collective-permute-start = (bf16[512,512]{1,0:T(8,128)(2,1)S(1)}, bf16[512,512]{1,0:T(8,128)(2,1)S(1)}, u32[]{:S(2)}, u32[]{:S(2)}) collective-permute-start(bf16[512,512]{1,0:T(8,128)(2,1)S(1)} %get-tuple-element.17.refs_1_), channel_id=1, source_target_pairs={{0,4},{1,5},{2,6},{3,7},{4,0},{5,1},{6,2},{7,3},{8,12},{9,13},{10,... | collective-permute-start | bytes 1572872 | tf_op jit(solution)/shard_map/ppermute | solution.py:290
  21.8 0.5 collective-permute-start.1
  22.3 0.0 collective-permute-start.4
  22.3 0.5 collective-permute-start.5
  22.8 0.0 copy-done.11
  22.8 0.0 copy-done.12
  22.8 0.0 copy-start.13
  22.8 9.0 %shard_map.146 = (f32[512,512]{1,0:T(8,128)}, f32[512,128]{1,0:T(8,128)}) custom-call(bf16[512,512]{1,0:T(8,128)(2,1)} %copy-done.10, bf16[512,512]{1,0:T(8,128)(2,1)} %copy-done.12, bf16[512,512]{1,0:T(8,128)(2,1)} %copy-done.11, bf16[512,512]{1,0:T(8,128)(2,1)} %refs_5_.1, bf16[512,512]{1,0:T(8,128)(2,1)} %refs_6_.1), custom_call_target="tpu_custom_call" | custom-call | flops 5368709120 | bytes 3145728 | tf_op jit(solution)/shard_map/pallas_call | solution.py:192
  31.8 0.2 collective-permute-done.refs_1_
  32.0 0.0 copy-start.16
  32.0 2.0 %collective-permute-done.1.refs_2_ = bf16[512,512]{1,0:T(8,128)(2,1)S(1)} collective-permute-done((bf16[512,512]{1,0:T(8,128)(2,1)S(1)}, bf16[512,512]{1,0:T(8,128)(2,1)S(1)}, u32[]{:S(2)}, u32[]{:S(2)}) %collective-permute-start.1) | collective-permute-done | bytes 524320 | tf_op jit(solution)/shard_map/ppermute | solution.py:290
  34.0 0.0 copy-start.17
  34.0 0.0 copy-start.15
  34.0 0.0 collective-permute-start.2
  34.0 0.5 collective-permute-start.3
  34.5 0.0 copy-done.13
  34.5 0.2 copy.17.w_out
  34.7 0.0 copy-done.15
  34.8 0.0 collective-permute-done.4.refs_1_
  34.8 0.0 collective-permute-done.5.refs_2_
  34.8 11.0 %shard_map.147 = (f32[512,512]{1,0:T(8,128)}, f32[512,128]{1,0:T(8,128)}) custom-call(bf16[512,512]{1,0:T(8,128)(2,1)} %copy-done.10, bf16[512,512]{1,0:T(8,128)(2,1)} %collective-permute-done.4.refs_1_, bf16[512,512]{1,0:T(8,128)(2,1)} %collective-permute-done.5.refs_2_, bf16[512,512]{1,0:T(8,128)(2,1)} %refs_5_.1, bf16[512,512]{1,0:T(8,128)(2,1)} %refs_6_.1, ...), custom_call_target="tpu_custom_call" | custom-call | flops 5368709120 | bytes 3145728 | tf_op jit(solution)/shard_map/pallas_call | solution.py:192
  45.7 0.0 copy-done.16
  45.7 0.0 copy-done.17
  45.7 0.0 collective-permute-done.2.refs_3_
  45.8 0.0 collective-permute-done.3.refs_4_
  45.8 0.0 copy-start.3
  45.8 0.0 copy-start.4
  45.8 0.0 copy-start.9
  45.8 17.1 %shard_map.148.packed = bf16[512,640]{1,0:T(8,128)(2,1)} custom-call(bf16[512,512]{1,0:T(8,128)(2,1)} %copy-done.10, bf16[512,512]{1,0:T(8,128)(2,1)} %copy-done.16, bf16[512,512]{1,0:T(8,128)(2,1)} %copy-done.17, bf16[512,512]{1,0:T(8,128)(2,1)} %collective-permute-done.2.refs_3_, bf16[512,512]{1,0:T(8,128)(2,1)} %collective-permute-done.3.refs_4_, ...), custom_call_target="tpu_custom_call" | custom-call | flops 10737418240 | bytes 4194304 | tf_op jit(solution)/shard_map/pallas_call | solution.py:192
  62.9 0.0 copy-start.8
  62.9 0.0 copy-done.3
  62.9 0.0 copy-done.4
  62.9 0.0 copy-done.9
  62.9 0.7 copy-done.8
  63.5 0.0 copy-start
  63.5 1.1 %copy-done = bf16[512,640]{1,0:T(8,128)(2,1)S(1)} copy-done((bf16[512,640]{1,0:T(8,128)(2,1)S(1)}, bf16[512,640]{1,0:T(8,128)(2,1)}, u32[]{:S(2)}) %copy-start) | copy-done | bytes 655384
  64.6 21.4 %shard_map.149 = f32[2,128]{1,0:T(2,128)S(1)} custom-call(bf16[512,640]{1,0:T(8,128)(2,1)S(1)} %copy-done, bf16[512,322]{1,0:T(8,128)(2,1)S(1)} %copy.17.w_out, f32[1,322]{1,0:T(1,128)S(1)} %reshape.18.mlp_gain, bf16[322,322]{1,0:T(8,128)(2,1)S(1)} %copy-done.3, bf16[322,322]{1,0:T(8,128)(2,1)S(1)} %copy-done.4, bf16[2,322]{1,0:T(2,128)(2,1)S(1)} %copy-done.8, ...), custom_call_target="tpu_custom_call" | custom-call | tf_op jit(solution)/shard_map/pallas_call | solution.py:339
  86.0 0.6 copy.19
  (2 shorter events, 0.0 us)
Async XLA Ops:
  0.0 1.3 %copy-start.14 = (f32[322]{0:T(512)S(1)}, f32[322]{0:T(512)}, u32[]{:S(2)}) copy-start(f32[322]{0:T(512)} %param.21) | copy-start | bytes 3868
  0.0 1.3 %copy-start.5 = (f32[64,322]{1,0:T(8,128)S(1)}, f32[64,322]{1,0:T(8,128)}, u32[]{:S(2)}) copy-start(f32[64,322]{1,0:T(8,128)} %table.1) | copy-start | bytes 247300
  0.0 1.3 %copy-start.1 = (bf16[512,512]{1,0:T(8,128)(2,1)S(1)}, bf16[512,512]{1,0:T(8,128)(2,1)}, u32[]{:S(2)}) copy-start(bf16[512,512]{1,0:T(8,128)(2,1)} %latents.1) | copy-start | bytes 1572868
  1.3 0.7 copy-start.7
  1.3 0.7 copy-start.6
  2.0 1.0 %copy-start.2 = (bf16[322,512]{1,0:T(8,128)(2,1)S(1)}, bf16[322,512]{1,0:T(8,128)(2,1)}, u32[]{:S(2)}) copy-start(bf16[322,512]{1,0:T(8,128)(2,1)} %w_query.1) | copy-start | bytes 989188
  19.5 0.8 copy-start.10
  20.3 2.5 %copy-start.11 = (bf16[512,512]{1,0:T(8,128)(2,1)}, bf16[512,512]{1,0:T(8,128)(2,1)S(1)}, u32[]{:S(2)}) copy-start(bf16[512,512]{1,0:T(8,128)(2,1)S(1)} %get-tuple-element.18.refs_2_) | copy-start | bytes 1572868
  20.3 2.5 %copy-start.12 = (bf16[512,512]{1,0:T(8,128)(2,1)}, bf16[512,512]{1,0:T(8,128)(2,1)S(1)}, u32[]{:S(2)}) copy-start(bf16[512,512]{1,0:T(8,128)(2,1)S(1)} %get-tuple-element.17.refs_1_) | copy-start | bytes 1572868
  20.3 11.7 %collective-permute-start = (bf16[512,512]{1,0:T(8,128)(2,1)S(1)}, bf16[512,512]{1,0:T(8,128)(2,1)S(1)}, u32[]{:S(2)}, u32[]{:S(2)}) collective-permute-start(bf16[512,512]{1,0:T(8,128)(2,1)S(1)} %get-tuple-element.17.refs_1_), channel_id=1, source_target_pairs={{0,4},{1,5},{2,6},{3,7},{4,0},{5,1},{6,2},{7,3},{8,12},{9,13},{10,... | collective-permute-start | bytes 1572872 | tf_op jit(solution)/shard_map/ppermute | solution.py:290
  21.8 12.2 %collective-permute-start.1 = (bf16[512,512]{1,0:T(8,128)(2,1)S(1)}, bf16[512,512]{1,0:T(8,128)(2,1)S(1)}, u32[]{:S(2)}, u32[]{:S(2)}) collective-permute-start(bf16[512,512]{1,0:T(8,128)(2,1)S(1)} %get-tuple-element.18.refs_2_), channel_id=1, source_target_pairs={{0,2},{1,3},{2,0},{3,1},{4,6},{5,7},{6,4},{7,5},{8,10},{9,11},{10,... | collective-permute-start | bytes 1572872 | tf_op jit(solution)/shard_map/ppermute | solution.py:290
  22.3 12.5 %collective-permute-start.4 = (bf16[512,512]{1,0:T(8,128)(2,1)S(1)}, bf16[512,512]{1,0:T(8,128)(2,1)}, u32[]{:S(2)}, u32[]{:S(2)}) collective-permute-start(bf16[512,512]{1,0:T(8,128)(2,1)S(1)} %get-tuple-element.17.refs_1_), channel_id=1, source_target_pairs={{0,1},{1,0},{2,3},{3,2},{4,5},{5,4},{6,7},{7,6},{8,9},{9,8},{10,11... | collective-permute-start | bytes 1572872 | tf_op jit(solution)/shard_map/ppermute | solution.py:290
  22.3 12.5 %collective-permute-start.5 = (bf16[512,512]{1,0:T(8,128)(2,1)S(1)}, bf16[512,512]{1,0:T(8,128)(2,1)}, u32[]{:S(2)}, u32[]{:S(2)}) collective-permute-start(bf16[512,512]{1,0:T(8,128)(2,1)S(1)} %get-tuple-element.18.refs_2_), channel_id=1, source_target_pairs={{0,1},{1,0},{2,3},{3,2},{4,5},{5,4},{6,7},{7,6},{8,9},{9,8},{10,11... | collective-permute-start | bytes 1572872 | tf_op jit(solution)/shard_map/ppermute | solution.py:290
  22.8 11.7 %copy-start.13 = (bf16[512,322]{0,1:T(8,128)(2,1)S(1)}, bf16[512,322]{0,1:T(8,128)(2,1)}, u32[]{:S(2)}) copy-start(bf16[512,322]{0,1:T(8,128)(2,1)} %param.25) | copy-start | bytes 989188
  32.0 13.7 %copy-start.16 = (bf16[512,512]{1,0:T(8,128)(2,1)}, bf16[512,512]{1,0:T(8,128)(2,1)S(1)}, u32[]{:S(2)}) copy-start(bf16[512,512]{1,0:T(8,128)(2,1)S(1)} %collective-permute-done.refs_1_) | copy-start | bytes 1572868
  34.0 11.7 %copy-start.17 = (bf16[512,512]{1,0:T(8,128)(2,1)}, bf16[512,512]{1,0:T(8,128)(2,1)S(1)}, u32[]{:S(2)}) copy-start(bf16[512,512]{1,0:T(8,128)(2,1)S(1)} %collective-permute-done.1.refs_2_) | copy-start | bytes 1572868
  34.0 0.7 copy-start.15
  34.0 11.7 %collective-permute-start.2 = (bf16[512,512]{1,0:T(8,128)(2,1)S(1)}, bf16[512,512]{1,0:T(8,128)(2,1)}, u32[]{:S(2)}, u32[]{:S(2)}) collective-permute-start(bf16[512,512]{1,0:T(8,128)(2,1)S(1)} %collective-permute-done.refs_1_), channel_id=1, source_target_pairs={{0,1},{1,0},{2,3},{3,2},{4,5},{5,4},{6,7},{7,6},{8,9},{9,8},{10,11... | collective-permute-start | bytes 1572872 | tf_op jit(solution)/shard_map/ppermute | solution.py:290
  34.0 11.7 %collective-permute-start.3 = (bf16[512,512]{1,0:T(8,128)(2,1)S(1)}, bf16[512,512]{1,0:T(8,128)(2,1)}, u32[]{:S(2)}, u32[]{:S(2)}) collective-permute-start(bf16[512,512]{1,0:T(8,128)(2,1)S(1)} %collective-permute-done.1.refs_2_), channel_id=1, source_target_pairs={{0,1},{1,0},{2,3},{3,2},{4,5},{5,4},{6,7},{7,6},{8,9},{9,8},{10,11... | collective-permute-start | bytes 1572872 | tf_op jit(solution)/shard_map/ppermute | solution.py:290
  45.8 17.1 %copy-start.3 = (bf16[322,322]{1,0:T(8,128)(2,1)S(1)}, bf16[322,322]{1,0:T(8,128)(2,1)}, u32[]{:S(2)}) copy-start(bf16[322,322]{1,0:T(8,128)(2,1)} %w_hidden.1) | copy-start | bytes 622108
  45.8 17.1 %copy-start.4 = (bf16[322,322]{1,0:T(8,128)(2,1)S(1)}, bf16[322,322]{1,0:T(8,128)(2,1)}, u32[]{:S(2)}) copy-start(bf16[322,322]{1,0:T(8,128)(2,1)} %w_back.1) | copy-start | bytes 622108
  45.8 17.1 %copy-start.9 = (s32[128]{0:T(128)S(1)}, s32[128]{0:T(128)}, u32[]{:S(2)}) copy-start(s32[128]{0:T(128)} %param.18) | copy-start | bytes 1540
  62.9 0.7 copy-start.8
  63.5 1.1 %copy-start = (bf16[512,640]{1,0:T(8,128)(2,1)S(1)}, bf16[512,640]{1,0:T(8,128)(2,1)}, u32[]{:S(2)}) copy-start(bf16[512,640]{1,0:T(8,128)(2,1)} %shard_map.148.packed) | copy-start | bytes 1966084

commit v4 on v3

--- a/solution.py
+++ b/solution.py
@@ -102,7 +102,7 @@
         q_out[k * share:(k + 1) * share, :] = q_got[k]
 
 
-def attend_kernel(pieces, first, last, *refs):
+def attend_kernel(pieces, first, last, *refs, tail=None):
     refs = list(refs)
     q_ref = refs.pop(0)
     lat_refs = [refs.pop(0) for _ in range(pieces)]
@@ -171,29 +171,30 @@
         else:
             new = jnp.where(low, kept, mixed)
             if last:
-                out[:, p * PAIR:(p + 1) * PAIR] = new.astype(BF)
+                out[p] = new.astype(BF)
+                tail(p)
             else:
                 acc_out[:, p * PAIR:(p + 1) * PAIR] = new
     if last:
-        out[:, PAIRS * PAIR:] = stats.astype(BF)
+        out[PAIRS] = stats.astype(BF)
+        tail(PAIRS)
     else:
         stat_out[...] = stats
 
 
-def attend(q, pieces, w_key, w_value, state, last):
+def attend(q, pieces, w_key, w_value, state):
     first = state is None
     rows = q.shape[0]
     count = sum(p.shape[0] for p in pieces)
     acc = jax.ShapeDtypeStruct((rows, PAIRS * PAIR), F32)
     stats = jax.ShapeDtypeStruct((rows, PAIR), F32)
-    packed = jax.ShapeDtypeStruct((rows, (PAIRS + 1) * PAIR), BF)
     args = [q, *pieces, w_key, w_value] + ([] if first else list(state))
     wide = w_key.shape[0]
     return pl.pallas_call(
-        functools.partial(attend_kernel, len(pieces), first, last),
-        out_shape=packed if last else (acc, stats),
+        functools.partial(attend_kernel, len(pieces), first, False),
+        out_shape=(acc, stats),
         in_specs=[VMEM] * len(args),
-        out_specs=VMEM if last else (VMEM, VMEM),
+        out_specs=(VMEM, VMEM),
         scratch_shapes=[
             pltpu.VMEM((PAIRS * PAIR, count), BF),
             pltpu.VMEM((PAIRS, count, 2 * PAIR), BF),
@@ -207,29 +208,35 @@
     )(*args)
 
 
-def finish_kernel(
-    outer, group, packed, w_out, mlp_gain, w_hidden, w_back, w_flow, valid, flow,
-    got, send_sem, recv_sem,
-):
+def finish_kernel(outer, group, pieces, *refs):
+    args = refs[:pieces + 5]
+    w_out, mlp_gain, w_hidden, w_back, w_flow, valid, flow = refs[pieces + 5:pieces + 12]
+    packed, got, keys, vals, send_sem, recv_sem = refs[pieces + 12:]
     ahead, across = peers(outer, group)
     greet([ahead(-k) for k in range(1, outer)])
-    rows = got.shape[1]
+    rows = got.shape[2]
     copies = []
-    for k in range(1, outer):
-        copy = pltpu.make_async_remote_copy(
-            src_ref=packed.at[pl.ds(k * rows, rows)], dst_ref=got.at[k],
-            send_sem=send_sem.at[k], recv_sem=recv_sem.at[k],
-            device_id=ahead(-k), device_id_type=MESH,
-        )
-        copy.start()
-        copies.append(copy)
+
+    def tail(p):
+        for k in range(1, outer):
+            copy = pltpu.make_async_remote_copy(
+                src_ref=packed.at[p, pl.ds(k * rows, rows)], dst_ref=got.at[p, k],
+                send_sem=send_sem.at[p, k], recv_sem=recv_sem.at[p, k],
+                device_id=ahead(-k), device_id_type=MESH,
+            )
+            copy.start()
+            copies.append(copy)
+
+    attend_kernel(pieces, False, True, *args, packed, keys, vals, tail=tail)
     for copy in copies:
         copy.wait()
-    part_refs = [packed.at[pl.ds(0, rows)]] + [got.at[k] for k in range(1, outer)]
-    wide = PAIRS * PAIR
+
+    def part(k, p):
+        return packed[p, :rows, :] if k == 0 else got[p, k]
+
     levels = []
-    for ref in part_refs:
-        st = ref[:, wide:].astype(F32)
+    for k in range(outer):
+        st = part(k, PAIRS).astype(F32)
         levels.append(
             st[:, :HEADS] + st[:, HEADS:2 * HEADS] + st[:, 2 * HEADS:3 * HEADS]
         )
@@ -241,9 +248,9 @@
     projected = jnp.zeros((rows, w_out.shape[1]), F32)
     for p in range(PAIRS):
         mixed = jnp.zeros((rows, PAIR), F32)
-        for ref, s in zip(part_refs, shares):
+        for k, s in enumerate(shares):
             weight = jnp.where(half, s[:, 2 * p:2 * p + 1], s[:, 2 * p + 1:2 * p + 2])
-            mixed = mixed + weight * ref[:, p * PAIR:(p + 1) * PAIR].astype(F32)
+            mixed = mixed + weight * part(k, p).astype(F32)
         projected = projected + jnp.dot(
             mixed.astype(BF), w_out[p * PAIR:(p + 1) * PAIR, :], preferred_element_type=F32
         )
@@ -324,7 +331,7 @@
     orders = [strides, strides[::-1]]
     near = [swap(piece, 1) for piece in held]
     far = [swap(held[c], orders[c][1 % len(strides)]) for c in range(2)]
-    state = attend(q, held, w_key, w_value, None, False)
+    state = attend(q, held, w_key, w_value, None)
     pending = near
     for j in range(1, len(strides)):
         far, state = lax.optimization_barrier((far, state))
@@ -333,24 +340,28 @@
         if j + 1 < len(strides):
             held = [jnp.concatenate([held[c], arrived[c]]) for c in range(2)]
             far = [swap(held[c], orders[c][j + 1]) for c in range(2)]
-        state = attend(q, pending, w_key, w_value, state, False)
+        state = attend(q, pending, w_key, w_value, state)
         pending = arrived + near
-    state = attend(q, pending, w_key, w_value, state, True)
+    count = sum(p.shape[0] for p in pending)
     return pl.pallas_call(
-        functools.partial(finish_kernel, outer, group),
+        functools.partial(finish_kernel, outer, group, len(pending)),
         out_shape=jax.ShapeDtypeStruct((w_flow.shape[0], share), F32),
-        in_specs=[VMEM] * 7,
+        in_specs=[VMEM] * (len(pending) + 11),
         out_specs=VMEM,
         scratch_shapes=[
-            pltpu.VMEM((outer, share, (PAIRS + 1) * PAIR), BF),
-            pltpu.SemaphoreType.DMA((outer,)),
-            pltpu.SemaphoreType.DMA((outer,)),
+            pltpu.VMEM((PAIRS + 1, outer * share, PAIR), BF),
+            pltpu.VMEM((PAIRS + 1, outer, share, PAIR), BF),
+            pltpu.VMEM((da, count), BF),
+            pltpu.VMEM((PAIRS, count, 2 * PAIR), BF),
+            pltpu.SemaphoreType.DMA((PAIRS + 1, outer)),
+            pltpu.SemaphoreType.DMA((PAIRS + 1, outer)),
         ],
         compiler_params=pltpu.CompilerParams(
-            collective_id=1, has_side_effects=True, vmem_limit_bytes=32 * 1024 * 1024
+            collective_id=1, has_side_effects=True, vmem_limit_bytes=56 * 1024 * 1024
         ),
     )(
-        state, w_out, mlp_gain.reshape(1, depth), w_hidden, w_back, w_flow,
+        q, *pending, w_key, w_value, *state,
+        w_out, mlp_gain.reshape(1, depth), w_hidden, w_back, w_flow,
         valid.reshape(1, share),
     )
 

time: 86.9 us -> 82 us (0.944)
  Pallas kernels: 74.9 us -> 68.4 us
  local copies, waits for them, and re-layouts: 6.27 us -> 7.94 us
    pallas_call x4 -> x3, Pallas kernels: 58.4 us -> 51.9 us  [the longest x1 32 us: local(): pl.pallas_call(functools.partial(finish_kernel, outer, group, len(pending...]
    unnamed x39 -> x33, local copies, waits for them, and re-layouts: 6.26 us -> 7.36 us
  transfers between devices with their start and end apart: 6 -> 6, of which waited for: 2 -> 2; matrix products, arithmetic and copies ran while one was open for 0% -> 2% of each run, Pallas kernels for 23% -> 24%
where the time goes in v4:
time: 82 us; the launch traced here: 81.8 us
  Pallas kernels  68.4 us (83%)
  local copies, waits for them, and re-layouts  7.94 us (10%)
  starting transfers between devices  3.01 us (4%)
  waiting for transfers between devices  2.27 us (3%)
    pallas_call x1, Pallas kernels, local(): pl.pallas_call(functools.partial(finish_kernel, outer, group, len(pending...  32 us
    pallas_call x2, Pallas kernels, attend(): pl.pallas_call(functools.partial(attend_kernel, len(pieces), first, False...  19.9 us
    pallas_call x1, Pallas kernels, local(): pl.pallas_call(functools.partial(prepare_kernel, outer, group, strides[0]...  16.5 us
    unnamed x33, local copies, waits for them, and re-layouts  7.36 us
    ppermute x6, starting transfers between devices, swap(): return lax.ppermute(value, both, pairs)  3.01 us
    ppermute x6, waiting for transfers between devices, swap(): return lax.ppermute(value, both, pairs)  2.27 us
  transfers between devices with their start and end apart: 6, of which 2 were waited for; matrix products, arithmetic and copies ran while one was open for 2% of the time, Pallas kernels for 24%

profile of v4, /device:TPU:0, one launch (start us, length us, event | category | flops | bytes accessed | tf_op | source)
XLA Modules:
  0.0 81.8 jit_solution(1042042135448872939)
XLA Ops:
  0.0 0.0 copy-start.12
  0.0 0.0 copy-start.3
  0.0 0.0 copy-start.1
  0.0 1.2 %copy.16.queries = bf16[512,322]{1,0:T(8,128)(2,1)S(1)} copy(bf16[512,322]{0,1:T(8,128)(2,1)} %param.15) | data formatting | bytes 659456 | tf_op args[0]
  1.3 0.0 copy-done.12
  1.3 0.0 copy-start.5
  1.3 0.0 copy-start.4
  1.3 0.0 copy-done.3
  1.3 0.0 copy-done.1
  1.3 0.6 copy-done.5
  2.0 0.0 copy-done.4
  2.0 0.0 copy-start.2
  2.0 1.0 %copy-done.2 = bf16[322,512]{1,0:T(8,128)(2,1)S(1)} copy-done((bf16[322,512]{1,0:T(8,128)(2,1)S(1)}, bf16[322,512]{1,0:T(8,128)(2,1)}, u32[]{:S(2)}) %copy-start.2) | copy-done | bytes 329752
  3.0 16.5 %shard_map.145 = (bf16[512,512]{1,0:T(8,128)(2,1)S(1)}, bf16[512,512]{1,0:T(8,128)(2,1)S(1)}, bf16[512,512]{1,0:T(8,128)(2,1)S(1)}) custom-call(bf16[512,322]{1,0:T(8,128)(2,1)S(1)} %copy.16.queries, s32[4,128]{1,0:T(4,128)S(1)} %bitcast.3, f32[64,322]{1,0:T(8,128)S(1)} %copy-done.3, bf16[512,512]{1,0:T(8,128)(2,1)S(1)} %copy-done.1, f32[1,512]{1,0:T(1,128)S(1)} %bitcast.4, ...), custom_call_target="tpu_custom_call" | custom-call | tf_op jit(solution)/shard_map/pallas_call | solution.py:303
  19.5 0.0 copy-start
  19.5 0.8 copy-done
  20.3 0.0 copy-start.6
  20.3 0.0 copy-start.7
  20.3 1.5 %collective-permute-start = (bf16[512,512]{1,0:T(8,128)(2,1)S(1)}, bf16[512,512]{1,0:T(8,128)(2,1)S(1)}, u32[]{:S(2)}, u32[]{:S(2)}) collective-permute-start(bf16[512,512]{1,0:T(8,128)(2,1)S(1)} %get-tuple-element.17.refs_1_), channel_id=1, source_target_pairs={{0,4},{1,5},{2,6},{3,7},{4,0},{5,1},{6,2},{7,3},{8,12},{9,13},{10,... | collective-permute-start | bytes 1572872 | tf_op jit(solution)/shard_map/ppermute | solution.py:297
  21.8 0.5 collective-permute-start.1
  22.3 0.0 collective-permute-start.4
  22.3 0.5 collective-permute-start.5
  22.8 0.0 copy-done.6
  22.8 0.0 copy-done.7
  22.8 0.0 copy-start.11
  22.8 8.9 %shard_map.146 = (f32[512,512]{1,0:T(8,128)}, f32[512,128]{1,0:T(8,128)}) custom-call(bf16[512,512]{1,0:T(8,128)(2,1)} %copy-done, bf16[512,512]{1,0:T(8,128)(2,1)} %copy-done.7, bf16[512,512]{1,0:T(8,128)(2,1)} %copy-done.6, bf16[512,512]{1,0:T(8,128)(2,1)} %refs_5_.1, bf16[512,512]{1,0:T(8,128)(2,1)} %refs_6_.1), custom_call_target="tpu_custom_call" | custom-call | flops 5368709120 | bytes 3145728 | tf_op jit(solution)/shard_map/pallas_call | solution.py:193
  31.7 0.3 collective-permute-done.refs_1_
  32.0 0.0 copy-start.8
  32.0 2.0 %collective-permute-done.1.refs_2_ = bf16[512,512]{1,0:T(8,128)(2,1)S(1)} collective-permute-done((bf16[512,512]{1,0:T(8,128)(2,1)S(1)}, bf16[512,512]{1,0:T(8,128)(2,1)S(1)}, u32[]{:S(2)}, u32[]{:S(2)}) %collective-permute-start.1) | collective-permute-done | bytes 524320 | tf_op jit(solution)/shard_map/ppermute | solution.py:297
  34.0 0.0 copy-start.9
  34.0 0.0 copy-start.13
  34.0 0.0 collective-permute-start.2
  34.0 0.5 collective-permute-start.3
  34.5 0.0 copy-done.11
  34.5 0.9 %copy.17.refs_9_ = bf16[512,322]{1,0:T(8,128)(2,1)} copy(bf16[512,322]{0,1:T(8,128)(2,1)S(1)} %copy-done.11) | data formatting | bytes 659456 | tf_op args[10]
  35.4 0.0 copy-done.13
  35.4 0.6 reshape.18.refs_10_
  36.0 0.0 collective-permute-done.4.refs_1_
  36.0 0.0 copy-start.14
  36.0 0.0 collective-permute-done.5.refs_2_
  36.0 0.8 copy-done.14
  36.8 11.0 %shard_map.147 = (f32[512,512]{1,0:T(8,128)}, f32[512,128]{1,0:T(8,128)}) custom-call(bf16[512,512]{1,0:T(8,128)(2,1)} %copy-done, bf16[512,512]{1,0:T(8,128)(2,1)} %copy-done.14, bf16[512,512]{1,0:T(8,128)(2,1)} %collective-permute-done.5.refs_2_, bf16[512,512]{1,0:T(8,128)(2,1)} %refs_5_.1, bf16[512,512]{1,0:T(8,128)(2,1)} %refs_6_.1, ...), custom_call_target="tpu_custom_call" | custom-call | flops 5368709120 | bytes 3145728 | tf_op jit(solution)/shard_map/pallas_call | solution.py:193
  47.8 0.0 copy-done.8
  47.8 0.0 copy-done.9
  47.8 0.0 collective-permute-done.2.refs_3_
  47.8 0.0 copy-start.10
  47.8 0.0 collective-permute-done.3.refs_4_
  47.8 0.8 copy-done.10
  48.6 32.0 %shard_map.148 = f32[2,128]{1,0:T(2,128)} custom-call(bf16[512,512]{1,0:T(8,128)(2,1)} %copy-done, bf16[512,512]{1,0:T(8,128)(2,1)} %copy-done.8, bf16[512,512]{1,0:T(8,128)(2,1)} %copy-done.9, bf16[512,512]{1,0:T(8,128)(2,1)} %copy-done.10, bf16[512,512]{1,0:T(8,128)(2,1)} %collective-permute-done.3.refs_4_, bf16[512,512]{1,0:T(8,128)(2,1)} %refs_5_.1, ...), custom_call_target="tpu_custom_call" | custom-call | tf_op jit(solution)/shard_map/pallas_call | solution.py:346
  80.6 1.2 %copy.19 = f32[2,128]{1,0:T(2,128)} copy(f32[2,128]{1,0:T(2,128)} %shard_map.148) | data formatting | bytes 2048
  (1 shorter events, 0.0 us)
Async XLA Ops:
  0.0 1.3 %copy-start.12 = (f32[322]{0:T(512)S(1)}, f32[322]{0:T(512)}, u32[]{:S(2)}) copy-start(f32[322]{0:T(512)} %param.21) | copy-start | bytes 3868
  0.0 1.3 %copy-start.3 = (f32[64,322]{1,0:T(8,128)S(1)}, f32[64,322]{1,0:T(8,128)}, u32[]{:S(2)}) copy-start(f32[64,322]{1,0:T(8,128)} %table.1) | copy-start | bytes 247300
  0.0 1.3 %copy-start.1 = (bf16[512,512]{1,0:T(8,128)(2,1)S(1)}, bf16[512,512]{1,0:T(8,128)(2,1)}, u32[]{:S(2)}) copy-start(bf16[512,512]{1,0:T(8,128)(2,1)} %latents.1) | copy-start | bytes 1572868
  1.3 0.7 copy-start.5
  1.3 0.7 copy-start.4
  2.0 1.0 %copy-start.2 = (bf16[322,512]{1,0:T(8,128)(2,1)S(1)}, bf16[322,512]{1,0:T(8,128)(2,1)}, u32[]{:S(2)}) copy-start(bf16[322,512]{1,0:T(8,128)(2,1)} %w_query.1) | copy-start | bytes 989188
  19.5 0.8 copy-start
  20.3 2.5 %copy-start.6 = (bf16[512,512]{1,0:T(8,128)(2,1)}, bf16[512,512]{1,0:T(8,128)(2,1)S(1)}, u32[]{:S(2)}) copy-start(bf16[512,512]{1,0:T(8,128)(2,1)S(1)} %get-tuple-element.18.refs_2_) | copy-start | bytes 1572868
  20.3 2.5 %copy-start.7 = (bf16[512,512]{1,0:T(8,128)(2,1)}, bf16[512,512]{1,0:T(8,128)(2,1)S(1)}, u32[]{:S(2)}) copy-start(bf16[512,512]{1,0:T(8,128)(2,1)S(1)} %get-tuple-element.17.refs_1_) | copy-start | bytes 1572868
  20.3 11.7 %collective-permute-start = (bf16[512,512]{1,0:T(8,128)(2,1)S(1)}, bf16[512,512]{1,0:T(8,128)(2,1)S(1)}, u32[]{:S(2)}, u32[]{:S(2)}) collective-permute-start(bf16[512,512]{1,0:T(8,128)(2,1)S(1)} %get-tuple-element.17.refs_1_), channel_id=1, source_target_pairs={{0,4},{1,5},{2,6},{3,7},{4,0},{5,1},{6,2},{7,3},{8,12},{9,13},{10,... | collective-permute-start | bytes 1572872 | tf_op jit(solution)/shard_map/ppermute | solution.py:297
  21.8 12.2 %collective-permute-start.1 = (bf16[512,512]{1,0:T(8,128)(2,1)S(1)}, bf16[512,512]{1,0:T(8,128)(2,1)S(1)}, u32[]{:S(2)}, u32[]{:S(2)}) collective-permute-start(bf16[512,512]{1,0:T(8,128)(2,1)S(1)} %get-tuple-element.18.refs_2_), channel_id=1, source_target_pairs={{0,2},{1,3},{2,0},{3,1},{4,6},{5,7},{6,4},{7,5},{8,10},{9,11},{10,... | collective-permute-start | bytes 1572872 | tf_op jit(solution)/shard_map/ppermute | solution.py:297
  22.3 13.8 %collective-permute-start.4 = (bf16[512,512]{1,0:T(8,128)(2,1)S(1)}, bf16[512,512]{1,0:T(8,128)(2,1)S(1)}, u32[]{:S(2)}, u32[]{:S(2)}) collective-permute-start(bf16[512,512]{1,0:T(8,128)(2,1)S(1)} %get-tuple-element.17.refs_1_), channel_id=1, source_target_pairs={{0,1},{1,0},{2,3},{3,2},{4,5},{5,4},{6,7},{7,6},{8,9},{9,8},{10,11... | collective-permute-start | bytes 1572872 | tf_op jit(solution)/shard_map/ppermute | solution.py:297
  22.3 13.8 %collective-permute-start.5 = (bf16[512,512]{1,0:T(8,128)(2,1)S(1)}, bf16[512,512]{1,0:T(8,128)(2,1)}, u32[]{:S(2)}, u32[]{:S(2)}) collective-permute-start(bf16[512,512]{1,0:T(8,128)(2,1)S(1)} %get-tuple-element.18.refs_2_), channel_id=1, source_target_pairs={{0,1},{1,0},{2,3},{3,2},{4,5},{5,4},{6,7},{7,6},{8,9},{9,8},{10,11... | collective-permute-start | bytes 1572872 | tf_op jit(solution)/shard_map/ppermute | solution.py:297
  22.8 11.7 %copy-start.11 = (bf16[512,322]{0,1:T(8,128)(2,1)S(1)}, bf16[512,322]{0,1:T(8,128)(2,1)}, u32[]{:S(2)}) copy-start(bf16[512,322]{0,1:T(8,128)(2,1)} %param.25) | copy-start | bytes 989188
  32.0 15.8 %copy-start.8 = (bf16[512,512]{1,0:T(8,128)(2,1)}, bf16[512,512]{1,0:T(8,128)(2,1)S(1)}, u32[]{:S(2)}) copy-start(bf16[512,512]{1,0:T(8,128)(2,1)S(1)} %collective-permute-done.refs_1_) | copy-start | bytes 1572868
  34.0 13.8 %copy-start.9 = (bf16[512,512]{1,0:T(8,128)(2,1)}, bf16[512,512]{1,0:T(8,128)(2,1)S(1)}, u32[]{:S(2)}) copy-start(bf16[512,512]{1,0:T(8,128)(2,1)S(1)} %collective-permute-done.1.refs_2_) | copy-start | bytes 1572868
  34.0 1.5 %copy-start.13 = (f32[322]{0:T(512)S(1)}, f32[322]{0:T(512)}, u32[]{:S(2)}) copy-start(f32[322]{0:T(512)} %param.26) | copy-start | bytes 3868
  34.0 13.8 %collective-permute-start.2 = (bf16[512,512]{1,0:T(8,128)(2,1)S(1)}, bf16[512,512]{1,0:T(8,128)(2,1)S(1)}, u32[]{:S(2)}, u32[]{:S(2)}) collective-permute-start(bf16[512,512]{1,0:T(8,128)(2,1)S(1)} %collective-permute-done.refs_1_), channel_id=1, source_target_pairs={{0,1},{1,0},{2,3},{3,2},{4,5},{5,4},{6,7},{7,6},{8,9},{9,8},{10,11... | collective-permute-start | bytes 1572872 | tf_op jit(solution)/shard_map/ppermute | solution.py:297
  34.0 13.8 %collective-permute-start.3 = (bf16[512,512]{1,0:T(8,128)(2,1)S(1)}, bf16[512,512]{1,0:T(8,128)(2,1)}, u32[]{:S(2)}, u32[]{:S(2)}) collective-permute-start(bf16[512,512]{1,0:T(8,128)(2,1)S(1)} %collective-permute-done.1.refs_2_), channel_id=1, source_target_pairs={{0,1},{1,0},{2,3},{3,2},{4,5},{5,4},{6,7},{7,6},{8,9},{9,8},{10,11... | collective-permute-start | bytes 1572872 | tf_op jit(solution)/shard_map/ppermute | solution.py:297
  36.0 0.8 copy-start.14
  47.8 0.8 copy-start.10
